TPU v7x, 32 devices: a whole 2x2x4 slice. The times are simulated.
32 devices in a mesh: groups: 2 (over x), role: 1, tp: 16 (over z, y, core).
Axes of the slice: x: 2, y: 2, z: 4, core: 2. Of those that a mesh axis runs over, the one named last changes fastest.
Arguments:
- queries: bfloat16 [4, 64, 16384], P(('groups', 'role'), None, 'tp'), parts along dimension 0, may hold values from -18 to 18
- cache_keys: bfloat16 [4, 16384, 1024], P(('groups', 'role'), 'tp'), parts along dimension 0, may hold values from -6 to 6
- cache_values: bfloat16 [4, 16384, 1024], P(('groups', 'role'), 'tp'), parts along dimension 0, may hold values from -6 to 6
- fresh_keys: bfloat16 [4, 64, 1024], P(('groups', 'role'), None, 'tp'), parts along dimension 0, may hold values from -12 to 12
- fresh_values: bfloat16 [4, 64, 1024], P(('groups', 'role'), None, 'tp'), parts along dimension 0, may hold values from -6 to 6
- prefill_prefixes: int32 [8], P('groups'), parts along dimension 0, may hold values from 1 to 6144, 16384 in all
- decode_prefixes: int32 [64], P('groups'), parts along dimension 0, may hold values from 1 to 8192, 16384 in all
- prefill_counts: int32 [8], P('groups'), parts along dimension 0, may hold values from 1 to 32, 64 in all
Outputs:
- attended: bfloat16 [4, 64, 16384], P(('groups', 'role'), None, 'tp'), parts along dimension 0
- handed_keys: bfloat16 [4, 64, 1024], P(('groups', 'role'), 'tp'), parts along dimension 0
- handed_values: bfloat16 [4, 64, 1024], P(('groups', 'role'), 'tp'), parts along dimension 0
There are 2 independent parts, one for each index of `groups`. A program takes and returns all parts, laid end to end along the dimension named above; each array names one. Nothing has to cross between parts.
Inputs may be any that keep to these rules, and one draw needn't show every extreme that they name: `prefill_prefixes`: the lengths sum to 16384 and the largest is exactly 6144; side 0's cache rows hold the prefill transcripts' prefixes one after another in order. `decode_prefixes`: the lengths sum to 16384 and the largest is exactly 8192; side 1's cache rows hold the decode transcripts' prefixes one after another in order. `prefill_counts`: the counts sum to 64 and the largest is exactly 32; side 0's query rows hold the turns in transcript order.
All inputs are finite; a program needn't handle non-finite values.
Results may differ from a plain program's by a relative error of at most 0.0039.
Values may be sent and summed in bfloat16 or wider, within the bound.
A program may use at most 128 MiB of HBM per device.

v0:
```python
import jax
import jax.numpy as jnp
from jax import lax
from jax.sharding import PartitionSpec as P

HEADS = 128
KV_HEADS = 8
HEAD_DIM = 128
GROUP_SIZE = 16


def passed_along(block, axis, distance):
    devices = range(lax.axis_size(axis))
    route = [((i - distance) % len(devices), i) for i in devices]
    return lax.ppermute(block, axis, route)


def owner_range(counts, start, length):
    ends = jnp.cumsum(counts)
    places = start + jnp.arange(length, dtype=jnp.int32)
    return jnp.sum((places[:, None] >= ends[None, :]).astype(jnp.int32), axis=1)


def masked_scores(grouped, key_block, visible):
    scores = jnp.einsum("qgad,kgd->gaqk", grouped, key_block, preferred_element_type=jnp.float32)
    scores = scores * HEAD_DIM ** (-0.5)
    return jnp.where(visible[None, None], scores, -1e30)


def shards(
    queries,
    cache_keys,
    cache_values,
    fresh_keys,
    fresh_values,
    prefill_prefixes,
    decode_prefixes,
    prefill_counts,
):
    device_place = lax.axis_index("tp")
    device_count = lax.axis_size("tp")
    side_place = lax.axis_index("role")
    local_sides = queries.shape[0]
    gathered = lax.all_gather(queries, "tp", axis=2, tiled=True)
    query_rows = gathered.shape[1]
    turn_keys, turn_values = (
        lax.all_to_all(fresh_keys, "tp", split_axis=1, concat_axis=2, tiled=True),
        lax.all_to_all(fresh_values, "tp", split_axis=1, concat_axis=2, tiled=True),
    )
    shifted_keys, shifted_values = passed_along((turn_keys, turn_values), "role", 1)
    handed_keys = jnp.flip(shifted_keys, axis=0)
    handed_values = jnp.flip(shifted_values, axis=0)
    query_places = jnp.arange(query_rows, dtype=jnp.int32)
    cache_rows = cache_keys.shape[1]
    cache_start = device_place * cache_rows
    turn_rows = turn_keys.shape[1]
    turn_places = device_place * turn_rows + jnp.arange(turn_rows, dtype=jnp.int32)
    block_rows = min(512, cache_rows)
    side_blocks = []
    side_grouped = []
    for local in range(local_sides):
        is_prefill = side_place * local_sides + local == 0
        query_owner = jnp.where(
            is_prefill, owner_range(prefill_counts, 0, query_rows), query_places // 2
        )
        cache_owner = jnp.where(
            is_prefill,
            owner_range(prefill_prefixes, cache_start, cache_rows),
            owner_range(decode_prefixes, cache_start, cache_rows),
        )
        turn_owner = jnp.where(
            is_prefill,
            owner_range(prefill_counts, device_place * turn_rows, turn_rows),
            turn_places // 2,
        )
        turn_visible = (query_owner[:, None] == turn_owner[None, :]) & (
            turn_places[None, :] <= query_places[:, None]
        )
        blocks = []
        for block_start in range(0, cache_rows, block_rows):
            key_block = cache_keys[local, block_start : block_start + block_rows].reshape(
                block_rows, KV_HEADS, HEAD_DIM
            )
            value_block = cache_values[local, block_start : block_start + block_rows].reshape(
                block_rows, KV_HEADS, HEAD_DIM
            )
            visible = (
                query_owner[:, None] == cache_owner[None, block_start : block_start + block_rows]
            )
            blocks.append((key_block, value_block, visible))
        blocks.append(
            (
                turn_keys[local].reshape(turn_rows, KV_HEADS, HEAD_DIM),
                turn_values[local].reshape(turn_rows, KV_HEADS, HEAD_DIM),
                turn_visible,
            )
        )
        side_blocks.append(blocks)
        side_grouped.append(gathered[local].reshape(query_rows, KV_HEADS, GROUP_SIZE, HEAD_DIM))
    maxima = []
    for local in range(local_sides):
        local_max = jnp.full((KV_HEADS, GROUP_SIZE, query_rows), -1e30, jnp.float32)
        for key_block, value_block, visible in side_blocks[local]:
            local_max = jnp.maximum(
                local_max, jnp.max(masked_scores(side_grouped[local], key_block, visible), axis=3)
            )
        maxima.append(local_max)
    row_max_all = lax.pmax(jnp.stack(maxima), "tp")
    numerators = []
    denominators = []
    for local in range(local_sides):
        row_max = row_max_all[local]
        numerator = jnp.zeros((query_rows, KV_HEADS, GROUP_SIZE, HEAD_DIM), jnp.float32)
        denominator = jnp.zeros((KV_HEADS, GROUP_SIZE, query_rows), jnp.float32)
        for key_block, value_block, visible in side_blocks[local]:
            weights = jnp.exp(
                masked_scores(side_grouped[local], key_block, visible) - row_max[..., None]
            )
            denominator = denominator + jnp.sum(weights, axis=3)
            numerator = numerator + jnp.einsum(
                "gaqk,kgd->qgad",
                weights.astype(jnp.bfloat16),
                value_block,
                preferred_element_type=jnp.float32,
            )
        numerators.append(numerator.reshape(query_rows, HEADS * HEAD_DIM))
        denominators.append(denominator.transpose(2, 0, 1).reshape(query_rows, HEADS))
    flat_numerator = jnp.stack(numerators)
    flat_denominator = jnp.stack(denominators)
    summed, totals = lax.psum((flat_numerator, flat_denominator), "tp")
    column_width = summed.shape[2] // device_count
    head_width = totals.shape[2] // device_count
    summed = lax.dynamic_slice_in_dim(summed, device_place * column_width, column_width, 2)
    totals = lax.dynamic_slice_in_dim(totals, device_place * head_width, head_width, 2)
    shares = summed.reshape(local_sides, query_rows, -1, HEAD_DIM) / totals[:, :, :, None]
    attended = shares.reshape(local_sides, query_rows, -1).astype(jnp.bfloat16)
    return (attended, handed_keys, handed_values)


def solution(mesh):
    return jax.shard_map(
        shards,
        mesh=mesh,
        in_specs=(
            P(("groups", "role"), None, "tp"),
            P(("groups", "role"), "tp", None),
            P(("groups", "role"), "tp", None),
            P(("groups", "role"), None, "tp"),
            P(("groups", "role"), None, "tp"),
            P("groups"),
            P("groups"),
            P("groups"),
        ),
        out_specs=(
            P(("groups", "role"), None, "tp"),
            P(("groups", "role"), "tp", None),
            P(("groups", "role"), "tp", None),
        ),
        check_vma=False,
    )
```

profile of v0, /device:TPU:3, one launch (start us, length us, event | category | flops | bytes accessed | tf_op | source)
XLA Modules:
  0.0 459.6 jit_solution(9744242315336176156)
XLA Ops:
  9.4 6.5 %all-to-all-start = ((bf16[16,2,256]{2,1,0:T(2,128)(2,1)}), bf16[16,2,256]{2,1,0:T(2,128)(2,1)S(1)}, u32[]{:S(2)}, u32[]{:S(2)}) async-start(bf16[16,2,256]{2,1,0:T(2,128)(2,1)} %reshape.417), calls=%async_computation | async-start | bytes 32768 | tf_op jit(solution)/shard_map/all_to_all | solution.py:47
  19.2 4.5 fusion.89
  23.7 2.1 fusion.88
  29.8 2.3 copy.156
  32.1 2.3 copy.157
  35.1 2.3 copy.154
  37.4 2.3 copy.155
  39.7 6.0 %all-to-all-start.1 = ((bf16[16,2,256]{2,1,0:T(2,128)(2,1)}), bf16[16,2,256]{2,1,0:T(2,128)(2,1)S(1)}, u32[]{:S(2)}, u32[]{:S(2)}) async-start(bf16[16,2,256]{2,1,0:T(2,128)(2,1)} %reshape.419), calls=%async_computation.1 | async-start | bytes 32768 | tf_op jit(solution)/shard_map/all_to_all | solution.py:48
  46.2 5.4 %all-to-all-done.1 = bf16[16,2,256]{2,1,0:T(2,128)(2,1)S(1)} async-done(((bf16[16,2,256]{2,1,0:T(2,128)(2,1)}), bf16[16,2,256]{2,1,0:T(2,128)(2,1)S(1)}, u32[]{:S(2)}, u32[]{:S(2)}) %all-to-all-start.1) | async-done | bytes 16416 | tf_op jit(solution)/shard_map/all_to_all | solution.py:48
  51.8 10.9 %all-gather.2.cloned.1.call-done = bf16[2,64,16384]{2,1,0:T(8,128)(2,1)} async-done(((bf16[2,64,1024]{2,1,0:T(8,128)(2,1)}), bf16[2,64,16384]{2,1,0:T(8,128)(2,1)}) %all-gather.2.cloned.1.call-update) | async-done | bytes 4194320 | tf_op jit(solution)/shard_map/all_gather | solution.py:44
  62.6 2.6 slice_bitcast_fusion.1
  66.4 2.5 fusion.94
  68.9 7.4 %fusion.11 = (f32[8,16,64]{2,1,0:T(8,128)S(1)}, f32[8,512,64,16]{1,2,3,0:T(8,128)}) fusion(pred[64,512]{1,0:T(8,128)(4,1)S(1)} %get-tuple-element.34, bf16[512,8,128,1]{0,2,3,1:T(8,128)(2,1)S(1)} %bitcast.176, bf16[64,8,16,128]{3,2,1,0:T(8,128)(2,1)S(1)} %bitcast.171), kind=kOutput, calls=%fused_computation.19 | convolution fusion | flops 1086316544 | bytes 19988480 | tf_op jit(solution)/shard_map/qgad,kgd->gaqk/dot_general | solution.py:25
  76.4 7.4 %fusion.10 = (f32[8,16,64]{2,1,0:T(8,128)S(1)}, f32[8,512,64,16]{1,2,3,0:T(8,128)}) fusion(pred[64,512]{1,0:T(8,128)(4,1)S(1)} %get-tuple-element.33, bf16[512,8,128,1]{0,2,3,1:T(8,128)(2,1)S(1)} %bitcast.175, bf16[64,8,16,128]{3,2,1,0:T(8,128)(2,1)S(1)} %bitcast.172), kind=kOutput, calls=%fused_computation.18 | convolution fusion | flops 1086316544 | bytes 19988480 | tf_op jit(solution)/shard_map/qgad,kgd->gaqk/dot_general | solution.py:25
  83.8 1.8 fusion.95
  85.5 7.5 %fusion.9 = (f32[8,16,64]{2,1,0:T(8,128)S(1)}, f32[8,512,64,16]{1,2,3,0:T(8,128)}) fusion(pred[64,512]{1,0:T(8,128)(4,1)S(1)} %get-tuple-element.30, bf16[512,8,128,1]{0,2,3,1:T(8,128)(2,1)S(1)} %bitcast.174, bf16[64,8,16,128]{3,2,1,0:T(8,128)(2,1)S(1)} %bitcast.168), kind=kOutput, calls=%fused_computation.17 | convolution fusion | flops 1086316544 | bytes 19988480 | tf_op jit(solution)/shard_map/qgad,kgd->gaqk/dot_general | solution.py:25
  93.0 7.4 %fusion.8 = (f32[8,16,64]{2,1,0:T(8,128)S(1)}, f32[8,512,64,16]{1,2,3,0:T(8,128)}) fusion(pred[64,512]{1,0:T(8,128)(4,1)S(1)} %get-tuple-element.29, bf16[512,8,128,1]{0,2,3,1:T(8,128)(2,1)S(1)} %bitcast.173, bf16[64,8,16,128]{3,2,1,0:T(8,128)(2,1)S(1)} %bitcast.169), kind=kOutput, calls=%fused_computation.16 | convolution fusion | flops 1086316544 | bytes 19988480 | tf_op jit(solution)/shard_map/qgad,kgd->gaqk/dot_general | solution.py:25
  101.6 85.4 %all-reduce.4.cloned.1.call-done = f32[2,8,16,64]{3,2,1,0:T(8,128)} async-done(((f32[2,8,16,64]{3,2,1,0:T(8,128)}), f32[2,8,16,64]{3,2,1,0:T(8,128)}) %all-reduce.4.cloned.1.call-update) | async-done | bytes 65552 | tf_op jit(solution)/shard_map/pmax | solution.py:108
  188.7 15.2 %fusion.6 = (f32[8,16,64]{2,1,0:T(8,128)}, f32[8,16,64]{2,1,0:T(8,128)}) fusion(f32[8,512,64,16]{1,2,3,0:T(8,128)} %get-tuple-element.38, f32[8,16,64]{2,1,0:T(8,128)S(1)} %get-tuple-element.20, pred[64,512]{1,0:T(8,128)(4,1)S(1)} %get-tuple-element.34, f32[8,512,64,16]{1,2,3,0:T(8,128)} %get-tuple-element.40, pred[64,512]{1,0:T(8,128)(4,1)S(1)} %get-tuple-element.33), kind=kLoop, calls=%fused_computation.14 | loop fusion | flops 33538048 | bytes 33718272 | tf_op jit(solution)/shard_map/reduce_sum | solution.py:119
  203.9 8.4 %fusion.14 = f32[8,16,64,128]{3,2,1,0:T(8,128)S(1)} fusion(bf16[512,8,128,1]{0,2,3,1:T(8,128)(2,1)S(1)} %bitcast.180, f32[8,512,64,16]{1,2,3,0:T(8,128)} %get-tuple-element.40, f32[8,16,64]{2,1,0:T(8,128)S(1)} %get-tuple-element.20, pred[64,512]{1,0:T(8,128)(4,1)S(1)} %get-tuple-element.33), kind=kOutput, calls=%fused_computation.21 | convolution fusion | flops 1090519040 | bytes 22085632 | tf_op jit(solution)/shard_map/gaqk,kgd->qgad/dot_general | solution.py:120
  212.4 5.3 %fusion.12 = f32[8,16,64,128]{3,2,1,0:T(8,128)S(1)} fusion(bf16[512,8,128,1]{0,2,3,1:T(8,128)(2,1)} %bitcast.179, f32[8,512,64,16]{1,2,3,0:T(8,128)S(1)} %bitcast.166, f32[8,16,64]{2,1,0:T(8,128)S(1)} %get-tuple-element.20, pred[64,512]{1,0:T(8,128)(4,1)S(1)} %get-tuple-element.34), kind=kOutput, calls=%fused_computation.20 | convolution fusion | flops 1090519040 | bytes 22085632 | tf_op jit(solution)/shard_map/gaqk,kgd->qgad/dot_general | solution.py:120
  217.7 1.8 add_bitcast_fusion
  219.5 4.4 copy.112
  223.9 5.0 %stack_reshape.13 = f32[1,64,16384]{2,1,0:T(8,128)} reshape(f32[64,8,16,128]{3,2,1,0:T(8,128)} %copy.112) | data formatting | bytes 8388608 | tf_op jit(solution)/shard_map/stack;reshape | solution.py:128
  229.7 14.5 %fusion.2 = (f32[8,16,64]{2,1,0:T(8,128)S(1)}, f32[8,16,64]{2,1,0:T(8,128)S(1)}) fusion(f32[8,512,64,16]{1,2,3,0:T(8,128)} %get-tuple-element.44, f32[8,16,64]{2,1,0:T(8,128)S(1)} %get-tuple-element.19, pred[64,512]{1,0:T(8,128)(4,1)S(1)} %get-tuple-element.30, f32[8,512,64,16]{1,2,3,0:T(8,128)} %get-tuple-element.46, pred[64,512]{1,0:T(8,128)(4,1)S(1)} %get-tuple-element.29), kind=kLoop, calls=%fused_computation.10 | loop fusion | flops 33538048 | bytes 33718272 | tf_op jit(solution)/shard_map/reduce_sum | solution.py:119
  244.3 8.3 %fusion.18 = f32[8,16,64,128]{3,2,1,0:T(8,128)S(1)} fusion(bf16[512,8,128,1]{0,2,3,1:T(8,128)(2,1)S(1)} %bitcast.178, f32[8,512,64,16]{1,2,3,0:T(8,128)} %get-tuple-element.46, f32[8,16,64]{2,1,0:T(8,128)S(1)} %get-tuple-element.19, pred[64,512]{1,0:T(8,128)(4,1)S(1)} %get-tuple-element.29), kind=kOutput, calls=%fused_computation.23 | convolution fusion | flops 1090519040 | bytes 22085632 | tf_op jit(solution)/shard_map/gaqk,kgd->qgad/dot_general | solution.py:120
  252.7 5.6 %fusion.16 = f32[8,16,64,128]{3,2,1,0:T(8,128)S(1)} fusion(bf16[512,8,128,1]{0,2,3,1:T(8,128)(2,1)} %bitcast.177, f32[8,512,64,16]{1,2,3,0:T(8,128)S(1)} %bitcast.164, f32[8,16,64]{2,1,0:T(8,128)S(1)} %get-tuple-element.19, pred[64,512]{1,0:T(8,128)(4,1)S(1)} %get-tuple-element.30), kind=kOutput, calls=%fused_computation.22 | convolution fusion | flops 1090519040 | bytes 22085632 | tf_op jit(solution)/shard_map/gaqk,kgd->qgad/dot_general | solution.py:120
  259.2 4.4 copy.106
  263.6 4.9 %stack_reshape.12 = f32[1,64,16384]{2,1,0:T(8,128)} reshape(f32[64,8,16,128]{3,2,1,0:T(8,128)} %copy.106) | data formatting | bytes 8388608 | tf_op jit(solution)/shard_map/stack;reshape | solution.py:128
  269.2 7.5 %pad_maximum_fusion = f32[2,64,16384]{2,1,0:T(8,128)} fusion(f32[1,64,16384]{2,1,0:T(8,128)} %stack_reshape.13, f32[1,64,16384]{2,1,0:T(8,128)} %stack_reshape.12), kind=kLoop, calls=%fused_computation.24 | loop fusion | flops 2097152 | bytes 16777216 | tf_op jit(solution)/shard_map/stack | solution.py:128
  278.2 171.9 %all-reduce.6.cloned.1.call-done = (f32[2,64,128]{1,2,0:T(8,128)}, f32[2,64,16384]{2,1,0:T(8,128)}) async-done(((f32[2,64,128]{1,2,0:T(8,128)}, f32[2,64,16384]{2,1,0:T(8,128)}), (f32[2,64,128]{1,2,0:T(8,128)}, f32[2,64,16384]{2,1,0:T(8,128)})) %all-reduce.6.cloned.1.call-update) | async-done | bytes 8454160 | tf_op jit(solution)/shard_map/psum | solution.py:130
  451.2 1.8 divide_convert_fusion
  (104 shorter events, 19.9 us)
Async XLA Ops:
  7.2 55.5 %all-gather.2.cloned.1.call-start = ((), (), s32[]{:S(2)}) async-start(), calls=%async_computation.2 | async-start | bytes 4456448 | tf_op jit(solution)/shard_map/all_gather | solution.py:44
  9.4 30.3 %all-to-all-start = ((bf16[16,2,256]{2,1,0:T(2,128)(2,1)}), bf16[16,2,256]{2,1,0:T(2,128)(2,1)S(1)}, u32[]{:S(2)}, u32[]{:S(2)}) async-start(bf16[16,2,256]{2,1,0:T(2,128)(2,1)} %reshape.417), calls=%async_computation | async-start | bytes 32768 | tf_op jit(solution)/shard_map/all_to_all | solution.py:47
  18.5 5.2 %copy-start.1 = (bf16[2,1024,1024]{2,1,0:T(8,128)(2,1)S(1)}, bf16[2,1024,1024]{2,1,0:T(8,128)(2,1)}, u32[]{:S(2)}) copy-start(bf16[2,1024,1024]{2,1,0:T(8,128)(2,1)} %param.10) | copy-start | bytes 12582916
  25.7 8.6 %copy-start.9 = (bf16[2,64,64]{2,1,0:T(8,128)(2,1)S(1)}, bf16[2,64,64]{2,1,0:T(8,128)(2,1)}, u32[]{:S(2)}) copy-start(bf16[2,64,64]{2,1,0:T(8,128)(2,1)} %param.12) | copy-start | bytes 49156
  39.7 12.0 %all-to-all-start.1 = ((bf16[16,2,256]{2,1,0:T(2,128)(2,1)}), bf16[16,2,256]{2,1,0:T(2,128)(2,1)S(1)}, u32[]{:S(2)}, u32[]{:S(2)}) async-start(bf16[16,2,256]{2,1,0:T(2,128)(2,1)} %reshape.419), calls=%async_computation.1 | async-start | bytes 32768 | tf_op jit(solution)/shard_map/all_to_all | solution.py:48
  45.7 141.3 %all-reduce.4.cloned.1.call-start = ((), (), s32[]{:S(2)}) async-start(), calls=%async_computation.3 | async-start | bytes 262144 | tf_op jit(solution)/shard_map/pmax | solution.py:108
  62.6 6.3 %copy-start = (bf16[1,512,1024]{1,2,0:T(8,128)(2,1)S(1)}, bf16[1,512,1024]{1,2,0:T(8,128)(2,1)}, u32[]{:S(2)}) copy-start(bf16[1,512,1024]{1,2,0:T(8,128)(2,1)} %copy.153) | copy-start | bytes 3145732
  93.0 94.9 %copy-start.2 = (f32[8,16,64,4]{2,3,1,0:T(4,128)S(1)}, f32[8,16,64,4]{2,3,1,0:T(4,128)}, u32[]{:S(2)}) copy-start(f32[8,16,64,4]{2,3,1,0:T(4,128)} %get-tuple-element.36) | copy-start | bytes 393220
  101.2 348.9 %all-reduce.6.cloned.1.call-start = ((), (), s32[]{:S(2)}) async-start(), calls=%async_computation.4 | async-start | bytes 17039360 | tf_op jit(solution)/shard_map/psum | solution.py:130
  188.7 15.2 %copy-start.4 = (bf16[1,512,1024]{1,2,0:T(8,128)(2,1)S(1)}, bf16[1,512,1024]{1,2,0:T(8,128)(2,1)}, u32[]{:S(2)}) copy-start(bf16[1,512,1024]{1,2,0:T(8,128)(2,1)} %copy.156) | copy-start | bytes 3145732
  188.7 23.6 %slice-start.4 = ((s8[16777216]{0:T(1024)(128)(4,1)}), s8[4194304]{0:T(1024)(128)(4,1)S(1)}, s32[]{:S(2)}) async-start(s8[16777216]{0:T(1024)(128)(4,1)} %bitcast.165), calls=%async_computation.9 | async-start | bytes 8388608
  188.7 23.6 %slice-start.5 = ((s8[16777216]{0:T(1024)(128)(4,1)}), s8[4194304]{0:T(1024)(128)(4,1)S(1)}, s32[]{:S(2)}) async-start(s8[16777216]{0:T(1024)(128)(4,1)} %bitcast.165), calls=%async_computation.10 | async-start | bytes 8388608
  188.7 23.6 %slice-start.6 = ((s8[16777216]{0:T(1024)(128)(4,1)}), s8[4194304]{0:T(1024)(128)(4,1)S(1)}, s32[]{:S(2)}) async-start(s8[16777216]{0:T(1024)(128)(4,1)} %bitcast.165), calls=%async_computation.11 | async-start | bytes 8388608
  203.9 8.4 %slice-start.7 = ((s8[16777216]{0:T(1024)(128)(4,1)}), s8[4194304]{0:T(1024)(128)(4,1)S(1)}, s32[]{:S(2)}) async-start(s8[16777216]{0:T(1024)(128)(4,1)} %bitcast.165), calls=%async_computation.12 | async-start | bytes 8388608
  229.7 14.6 %copy-start.3 = (bf16[1,512,1024]{1,2,0:T(8,128)(2,1)S(1)}, bf16[1,512,1024]{1,2,0:T(8,128)(2,1)}, u32[]{:S(2)}) copy-start(bf16[1,512,1024]{1,2,0:T(8,128)(2,1)} %copy.154) | copy-start | bytes 3145732
  229.7 22.9 %slice-start = ((s8[16777216]{0:T(1024)(128)(4,1)}), s8[4194304]{0:T(1024)(128)(4,1)S(1)}, s32[]{:S(2)}) async-start(s8[16777216]{0:T(1024)(128)(4,1)} %bitcast.163), calls=%async_computation.5 | async-start | bytes 8388608
  229.7 22.9 %slice-start.1 = ((s8[16777216]{0:T(1024)(128)(4,1)}), s8[4194304]{0:T(1024)(128)(4,1)S(1)}, s32[]{:S(2)}) async-start(s8[16777216]{0:T(1024)(128)(4,1)} %bitcast.163), calls=%async_computation.6 | async-start | bytes 8388608
  229.7 22.9 %slice-start.2 = ((s8[16777216]{0:T(1024)(128)(4,1)}), s8[4194304]{0:T(1024)(128)(4,1)S(1)}, s32[]{:S(2)}) async-start(s8[16777216]{0:T(1024)(128)(4,1)} %bitcast.163), calls=%async_computation.7 | async-start | bytes 8388608
  244.3 8.4 %slice-start.3 = ((s8[16777216]{0:T(1024)(128)(4,1)}), s8[4194304]{0:T(1024)(128)(4,1)S(1)}, s32[]{:S(2)}) async-start(s8[16777216]{0:T(1024)(128)(4,1)} %bitcast.163), calls=%async_computation.8 | async-start | bytes 8388608
  259.2 9.3 %copy-start.5 = (f32[8,16,64]{2,1,0:T(8,128)S(1)}, f32[8,16,64]{2,1,0:T(8,128)}, u32[]{:S(2)}) copy-start(f32[8,16,64]{2,1,0:T(8,128)} %get-tuple-element.5) | copy-start | bytes 98308
  259.2 9.3 %copy-start.6 = (f32[8,16,64]{2,1,0:T(8,128)S(1)}, f32[8,16,64]{2,1,0:T(8,128)}, u32[]{:S(2)}) copy-start(f32[8,16,64]{2,1,0:T(8,128)} %get-tuple-element.6) | copy-start | bytes 98308
  259.2 9.3 %copy-start.7 = (f32[8,16,64]{2,1,0:T(8,128)S(1)}, f32[8,16,64]{2,1,0:T(8,128)}, u32[]{:S(2)}) copy-start(f32[8,16,64]{2,1,0:T(8,128)} %fusion.68) | copy-start | bytes 98308
  259.2 9.3 %copy-start.8 = (f32[8,16,64]{2,1,0:T(8,128)S(1)}, f32[8,16,64]{2,1,0:T(8,128)}, u32[]{:S(2)}) copy-start(f32[8,16,64]{2,1,0:T(8,128)} %fusion.66) | copy-start | bytes 98308
  276.9 0.1 collective-permute-start
  277.0 0.6 collective-permute-start.1
Sparse Core Ops, SparseCore 0:
  10.2 52.3 all-gather.1
  101.3 85.6 all-reduce.3
  276.9 173.1 all-reduce.5
where the time goes:
time: 462 us; the launch traced here: 460 us
  waiting for transfers between devices  274 us (59%)
  matrix products  64.3 us (14%)
  local copies, waits for them, and re-layouts  49.1 us (11%)
  other arithmetic  44.7 us (10%)
  between operations  14.2 us (3%)
  starting transfers between devices  13.1 us (3%)
    psum x1, waiting for transfers between devices, shards(): summed, totals = lax.psum((flat_numerator, flat_denominator), 'tp')  172 us
    pmax x1, waiting for transfers between devices, shards(): row_max_all = lax.pmax(jnp.stack(maxima), 'tp')  85.4 us
    dot_general x6, matrix products, masked_scores(): jnp.einsum('qgad,kgd->gaqk', grouped, key_block, preferred_element_type=j...  34 us
    reduce_sum x4, other arithmetic, shards(): denominator = denominator + jnp.sum(weights, axis=3)  31.4 us
    dot_general x6, matrix products, shards(): jnp.einsum('gaqk,kgd->qgad', weights.astype(jnp.bfloat16), value_block, p...  30.3 us
    unnamed x53, local copies, waits for them, and re-layouts  19.4 us
    all_gather x1, waiting for transfers between devices, shards(): gathered = lax.all_gather(queries, 'tp', axis=2, tiled=True)  10.9 us
    another operation x2, local copies, waits for them, and re-layouts, shards(): flat_numerator = jnp.stack(numerators)  9.93 us
  transfers between devices with their start and end apart: 7, of which 4 were waited for; matrix products, arithmetic and copies ran while one was open for 6% of the time, Pallas kernels for 0%

commit v1 on v0

--- a/solution.py
+++ b/solution.py
@@ -1,6 +1,8 @@
 import jax
 import jax.numpy as jnp
 from jax import lax
+from jax.experimental import pallas as pl
+from jax.experimental.pallas import tpu as pltpu
 from jax.sharding import PartitionSpec as P
 
 HEADS = 128
@@ -136,10 +138,410 @@
     attended = shares.reshape(local_sides, query_rows, -1).astype(jnp.bfloat16)
     return (attended, handed_keys, handed_values)
 
+TP = 16
+ZS = 4
+BLOCK = 512
+TILES = 4
+HEADS_PER_STEP = 2
+SCALE = HEAD_DIM ** (-0.5)
+MESH = pl.DeviceIdType.MESH
+LIMIT = 48 * 1024 * 1024
+
+
+def place(z, y, c):
+    return (z * 2 + y) * 2 + c
+
+
+def greet(me):
+    barrier = pltpu.get_barrier_semaphore()
+    for d in range(1, TP):
+        pl.semaphore_signal(
+            barrier, inc=1, device_id={"tp": lax.rem(me + d, TP)}, device_id_type=MESH
+        )
+    pl.semaphore_wait(barrier, TP - 1)
+
+
+def remote(src, dst, send, recv, to):
+    return pltpu.make_async_remote_copy(
+        src_ref=src, dst_ref=dst, send_sem=send, recv_sem=recv,
+        device_id={"tp": to}, device_id_type=MESH,
+    )
+
+
+def gather_kernel(q_ref, f_ref, out_ref, fout_ref, send, recv, fsend, frecv, local):
+    me = lax.axis_index("tp")
+    c, y, z = lax.rem(me, 2), lax.rem(me // 2, 2), me // 4
+    other_y, other_c = place(z, 1 - y, c), place(z, y, 1 - c)
+    greet(me)
+    own = [
+        pltpu.make_async_copy(q_ref, out_ref.at[me], local.at[0]),
+        pltpu.make_async_copy(f_ref.at[me], fout_ref.at[me], local.at[1]),
+    ]
+    for copy in own:
+        copy.start()
+    sends = []
+
+    def push(src, origin, s, to):
+        copy = remote(
+            src, out_ref.at[origin, s], send.at[len(sends)], recv.at[origin * 2 + s], to
+        )
+        copy.start()
+        sends.append(copy)
+
+    def arrived(origin, s):
+        remote(
+            out_ref.at[origin, s], out_ref.at[origin, s], send.at[0],
+            recv.at[origin * 2 + s], other_c,
+        ).wait_recv()
+
+    for s in range(2):
+        for dz in (2, 1, 3):
+            push(q_ref.at[s], me, s, place(lax.rem(z + dz, ZS), y, c))
+        push(q_ref.at[s], me, s, other_y)
+        push(q_ref.at[s], me, s, other_c)
+    fresh = []
+    for d in range(1, TP):
+        to = lax.rem(me + d, TP)
+        copy = remote(f_ref.at[to], fout_ref.at[me], fsend.at[d], frecv.at[d], to)
+        copy.start()
+        fresh.append(copy)
+    for s in range(2):
+        for dz in (1, 3, 2):
+            origin = place(lax.rem(z + dz, ZS), y, c)
+            arrived(origin, s)
+            push(out_ref.at[origin, s], origin, s, other_y)
+            push(out_ref.at[origin, s], origin, s, other_c)
+    for s in range(2):
+        for dz in (0, 1, 3, 2):
+            origin = place(lax.rem(z + dz, ZS), 1 - y, c)
+            arrived(origin, s)
+            push(out_ref.at[origin, s], origin, s, other_c)
+    for s in range(2):
+        for row in range(2):
+            for dz in range(ZS):
+                arrived(place(lax.rem(z + dz, ZS), row, 1 - c), s)
+    for d in range(1, TP):
+        src = lax.rem(me - d + TP, TP)
+        remote(f_ref.at[src], fout_ref.at[src], fsend.at[d], frecv.at[d], src).wait_recv()
+    for copy in sends + fresh:
+        copy.wait_send()
+    for copy in own:
+        copy.wait()
+
+
+def max_kernel(m_ref, out_ref, slots, send, recv, send2, recv2):
+    me = lax.axis_index("tp")
+    greet(me)
+    first, second = [], []
+    for d in range(1, TP):
+        to = lax.rem(me + d, TP)
+        copy = remote(m_ref.at[to], slots.at[d - 1], send.at[d], recv.at[d], to)
+        copy.start()
+        first.append(copy)
+    best = m_ref[me]
+    for d in range(1, TP):
+        first[d - 1].wait_recv()
+        best = jnp.maximum(best, slots[d - 1])
+    out_ref[me] = best
+    for d in range(1, TP):
+        to = lax.rem(me + d, TP)
+        copy = remote(out_ref.at[me], out_ref.at[me], send2.at[d], recv2.at[d], to)
+        copy.start()
+        second.append(copy)
+    for d in range(1, TP):
+        src = lax.rem(me - d + TP, TP)
+        remote(
+            out_ref.at[src], out_ref.at[src], send2.at[d], recv2.at[d], src
+        ).wait_recv()
+    for copy in first + second:
+        copy.wait_send()
+
+
+def reduce_kernel(
+    num_ref, l_ref, out_ref, c_in, y_out, y_in, z_out, z_in, l_in,
+    c_send, c_recv, y_send, y_recv, z_send, z_recv, l_send, l_recv,
+):
+    me = lax.axis_index("tp")
+    c, y, z = lax.rem(me, 2), lax.rem(me // 2, 2), me // 4
+    other_y, other_c = place(z, 1 - y, c), place(z, y, 1 - c)
+    greet(me)
+    c_copies, y_copies, z_copies, l_copies = {}, {}, {}, []
+    for s in range(2):
+        for near in range(2):
+            row = y if near else 1 - y
+            for dz in range(ZS):
+                to_z = lax.rem(z + dz, ZS)
+                at = (s * 2 + near) * ZS + dz
+                copy = remote(
+                    num_ref.at[place(to_z, row, 1 - c), s], c_in.at[at],
+                    c_send.at[at], c_recv.at[at], other_c,
+                )
+                copy.start()
+                c_copies[at] = copy
+    for d in range(1, TP):
+        to = lax.rem(me + d, TP)
+        copy = remote(l_ref.at[to], l_in.at[d - 1], l_send.at[d], l_recv.at[d], to)
+        copy.start()
+        l_copies.append(copy)
+    order = (2, 1, 3, 0)
+    for s in range(2):
+        for dz in order:
+            at, slot = s * 2 * ZS + dz, s * ZS + dz
+            c_copies[at].wait_recv()
+            dest = place(lax.rem(z + dz, ZS), 1 - y, c)
+            y_out[slot] = (num_ref[dest, s] + c_in[at]).astype(jnp.bfloat16)
+            copy = remote(
+                y_out.at[slot], y_in.at[slot], y_send.at[slot], y_recv.at[slot], other_y
+            )
+            copy.start()
+            y_copies[slot] = copy
+    kept = []
+    for s in range(2):
+        for dz in order:
+            at, slot = (s * 2 + 1) * ZS + dz, s * ZS + dz
+            c_copies[at].wait_recv()
+            y_copies[slot].wait_recv()
+            to = place(lax.rem(z + dz, ZS), y, c)
+            total = num_ref[to, s] + c_in[at] + y_in[slot].astype(jnp.float32)
+            if dz == 0:
+                c_in[at] = total
+            else:
+                z_out[slot] = total.astype(jnp.bfloat16)
+                copy = remote(
+                    z_out.at[slot], z_in.at[slot], z_send.at[slot], z_recv.at[slot], to
+                )
+                copy.start()
+                z_copies[slot] = copy
+    totals = l_ref[me]
+    for d in range(1, TP):
+        l_copies[d - 1].wait_recv()
+        totals = totals + l_in[d - 1]
+    columns = totals.T
+    for s in range(2):
+        for dz in (1, 3, 2):
+            z_copies[s * ZS + dz].wait_recv()
+        for j in range(TILES):
+            rows = slice(128 * j, 128 * j + 128)
+            total = c_in[(s * 2 + 1) * ZS, rows]
+            for dz in range(1, ZS):
+                total = total + z_in[s * ZS + dz, rows].astype(jnp.float32)
+            at = s * TILES + j
+            out_ref[s, rows] = (total / columns[:, at : at + 1]).astype(jnp.bfloat16)
+    for copy in [*c_copies.values(), *y_copies.values(), *z_copies.values(), *l_copies]:
+        copy.wait_send()
+
+
+def scores_of(q_ref, k_ref, bound_ref, h, j, kind, block):
+    q = q_ref[h, :, 0, 128 * j : 128 * j + 128, :].reshape(256, HEAD_DIM)
+    rows = BLOCK if kind == 0 else k_ref.shape[1]
+    k = k_ref[0, rows * block : rows * block + rows, HEAD_DIM * h : HEAD_DIM * h + HEAD_DIM]
+    s = lax.dot_general(
+        k, q, (((1,), (1,)), ((), ())), preferred_element_type=jnp.float32
+    )
+    at = lax.broadcasted_iota(jnp.int32, s.shape, 0)
+    low = bound_ref[0, j, 2 * kind : 2 * kind + 1, :] - rows * block
+    high = bound_ref[0, j, 2 * kind + 1 : 2 * kind + 2, :] - rows * block
+    return jnp.where((at >= low) & (at < high), s, -1e30)
+
+
+def pieces(k_ref):
+    count = k_ref.shape[1] // BLOCK
+    return [(0, b) for b in range(count)] + [(1, 0)]
+
+
+def local_max_kernel(flag_ref, q_ref, k_ref, t_ref, bound_ref, m_ref):
+    side = pl.program_id(0)
+    m_ref[...] = jnp.full(m_ref.shape, -1e30, jnp.float32)
+    parts = pieces(k_ref)
+    for j in range(TILES):
+        for n, (kind, block) in enumerate(parts):
+            @pl.when(flag_ref[(side * len(parts) + n) * TILES + j] != 0)
+            def _():
+                for h in range(HEADS_PER_STEP):
+                    s = scores_of(q_ref, t_ref if kind else k_ref, bound_ref, h, j, kind, block)
+                    top = jnp.max(s, axis=0, keepdims=True)
+                    for p in range(2):
+                        row = m_ref[h, p, 0, j : j + 1, :]
+                        m_ref[h, p, 0, j : j + 1, :] = jnp.maximum(
+                            row, top[:, 128 * p : 128 * p + 128]
+                        )
+
+
+def weigh_kernel(
+    flag_ref, q_ref, k_ref, v_ref, t_ref, u_ref, bound_ref, m_ref, num_ref, l_ref, total
+):
+    side = pl.program_id(0)
+    l_ref[...] = jnp.zeros(l_ref.shape, jnp.float32)
+    parts = pieces(k_ref)
+    for j in range(TILES):
+        total[...] = jnp.zeros_like(total)
+        for n, (kind, block) in enumerate(parts):
+            @pl.when(flag_ref[(side * len(parts) + n) * TILES + j] != 0)
+            def _():
+                for h in range(HEADS_PER_STEP):
+                    s = scores_of(q_ref, t_ref if kind else k_ref, bound_ref, h, j, kind, block)
+                    top = jnp.concatenate(
+                        [m_ref[h, p, 0, j : j + 1, :] for p in range(2)], axis=1
+                    )
+                    w = jnp.exp((s - top) * SCALE)
+                    sums = jnp.sum(w, axis=0, keepdims=True)
+                    for p in range(2):
+                        l_ref[h, p, 0, j : j + 1, :] += sums[:, 128 * p : 128 * p + 128]
+                    rows = s.shape[0]
+                    v = (u_ref if kind else v_ref)[
+                        0, rows * block : rows * block + rows,
+                        HEAD_DIM * h : HEAD_DIM * h + HEAD_DIM,
+                    ]
+                    total[h] += lax.dot_general(
+                        v, w.astype(jnp.bfloat16), (((0,), (0,)), ((), ())),
+                        preferred_element_type=jnp.float32,
+                    )
+        for h in range(HEADS_PER_STEP):
+            done = total[h].T
+            for p in range(2):
+                num_ref[h, p, 0, 128 * j : 128 * j + 128, :] = done[128 * p : 128 * p + 128]
+
+
+def spans(counts, owner):
+    t = jnp.arange(counts.shape[0], dtype=jnp.int32)
+    start = jnp.sum(jnp.where(t[None] < owner[:, None], counts[None], 0), axis=1)
+    return start, start + jnp.sum(jnp.where(t[None] == owner[:, None], counts[None], 0), axis=1)
+
+
+def fast_shards(
+    queries,
+    cache_keys,
+    cache_values,
+    fresh_keys,
+    fresh_values,
+    prefill_prefixes,
+    decode_prefixes,
+    prefill_counts,
+):
+    me = lax.axis_index("tp")
+    query_rows = queries.shape[1]
+    cache_rows = cache_keys.shape[1]
+    turn_rows = query_rows // TP
+    q = queries.reshape(2, query_rows * 8, HEAD_DIM)
+    fresh = jnp.stack([fresh_keys, fresh_values]).reshape(2, 2, TP, turn_rows, -1)
+    fresh = fresh.transpose(2, 0, 1, 3, 4).reshape(TP, 4 * turn_rows, -1)
+    fresh = jnp.pad(fresh, ((0, 0), (0, 0), (0, 64)))
+    any_spec = pl.BlockSpec(memory_space=pl.ANY)
+    vmem_spec = pl.BlockSpec(memory_space=pltpu.VMEM)
+    dma = pltpu.SemaphoreType.DMA
+    gathered, turns = pl.pallas_call(
+        gather_kernel,
+        out_shape=(
+            jax.ShapeDtypeStruct((TP, *q.shape), jnp.bfloat16),
+            jax.ShapeDtypeStruct(fresh.shape, jnp.bfloat16),
+        ),
+        in_specs=[any_spec] * 2,
+        out_specs=(any_spec, any_spec),
+        scratch_shapes=[dma((32,)), dma((32,)), dma((TP,)), dma((TP,)), dma((2,))],
+        compiler_params=pltpu.CompilerParams(collective_id=0, has_side_effects=True),
+        name="gather_queries",
+    )(q, fresh)
+    turns = turns[:, :, :64].reshape(TP, 2, 2, turn_rows, 64)
+    turns = turns.transpose(1, 2, 3, 0, 4).reshape(2, 2, turn_rows, -1)
+    handed_keys, handed_values = jnp.flip(turns[0], axis=0), jnp.flip(turns[1], axis=0)
+    padded = jnp.pad(turns, ((0, 0), (0, 0), (0, 16 - turn_rows), (0, 0)))
+
+    places = jnp.arange(query_rows, dtype=jnp.int32)
+    t = jnp.arange(prefill_counts.shape[0], dtype=jnp.int32)
+    ends = jnp.sum(jnp.where(t[None] <= t[:, None], prefill_counts[None], 0), axis=1)
+    owner = jnp.sum((places[:, None] >= ends[None]).astype(jnp.int32), axis=1)
+    turn_start = spans(prefill_counts, owner)[0]
+    start, end = zip(spans(prefill_prefixes, owner), spans(decode_prefixes, places // 2))
+    cache_start, cache_end = jnp.stack(start), jnp.stack(end)
+    turn_start = jnp.stack([turn_start, places // 2 * 2])
+    turn_end = jnp.broadcast_to(places + 1, (2, query_rows))
+    cache_start, cache_end = cache_start - me * cache_rows, cache_end - me * cache_rows
+    turn_start = turn_start - me * turn_rows
+    turn_end = jnp.minimum(turn_end - me * turn_rows, turn_rows)
+    bounds = jnp.stack([cache_start, cache_end, turn_start, turn_end], axis=1)
+    tiled = bounds.reshape(2, 4, TILES, query_rows // TILES).transpose(0, 2, 1, 3)
+    wide = jnp.broadcast_to(
+        tiled[:, :, :, None, :, None], (2, TILES, 4, 2, query_rows // TILES, 8)
+    ).reshape(2, TILES, 4, 256)
+    flags = []
+    for b in range(cache_rows // BLOCK):
+        flags.append((tiled[:, :, 0] < (b + 1) * BLOCK) & (tiled[:, :, 1] > b * BLOCK))
+    flags.append((tiled[:, :, 2] < tiled[:, :, 3]) & (tiled[:, :, 3] > 0))
+    flags = jnp.any(jnp.stack(flags, axis=1), axis=-1).astype(jnp.int32).reshape(-1)
+
+    hs = HEADS_PER_STEP
+    smem = pl.BlockSpec(memory_space=pltpu.SMEM)
+    q_spec = pl.BlockSpec((hs, 2, 1, 512, HEAD_DIM), lambda s, g: (g, 0, s, 0, 0))
+    n_spec = pl.BlockSpec((hs, 2, 1, 512, HEAD_DIM), lambda s, g: (g, 0, s, 0, 0))
+    k_spec = pl.BlockSpec((1, cache_rows, hs * HEAD_DIM), lambda s, g: (s, 0, g))
+    t_spec = pl.BlockSpec((1, 16, hs * HEAD_DIM), lambda s, g: (s, 0, g))
+    b_spec = pl.BlockSpec((1, TILES, 4, 256), lambda s, g: (s, 0, 0, 0))
+    m_spec = pl.BlockSpec((hs, 2, 1, TILES, 128), lambda s, g: (g, 0, s, 0, 0))
+    stats = jax.ShapeDtypeStruct((KV_HEADS, 2, 2, TILES, 128), jnp.float32)
+    grid = (2, KV_HEADS // hs)
+    params = pltpu.CompilerParams(vmem_limit_bytes=LIMIT)
+    gathered = gathered.reshape(KV_HEADS, 2, *q.shape)
+    local_max = pl.pallas_call(
+        local_max_kernel,
+        grid=grid,
+        out_shape=stats,
+        in_specs=[smem, q_spec, k_spec, t_spec, b_spec],
+        out_specs=m_spec,
+        compiler_params=params,
+        name="local_max",
+    )(flags, gathered, cache_keys, padded[0], wide)
+    row_max = pl.pallas_call(
+        max_kernel,
+        out_shape=jax.ShapeDtypeStruct((TP, 8, 128), jnp.float32),
+        in_specs=[vmem_spec],
+        out_specs=vmem_spec,
+        scratch_shapes=[pltpu.VMEM((TP - 1, 8, 128), jnp.float32)] + [dma((TP,))] * 4,
+        compiler_params=pltpu.CompilerParams(collective_id=1, has_side_effects=True),
+        name="row_max",
+    )(local_max.reshape(TP, 8, 128))
+    numerator, denominator = pl.pallas_call(
+        weigh_kernel,
+        grid=grid,
+        out_shape=(
+            jax.ShapeDtypeStruct((KV_HEADS, 2, 2, 512, HEAD_DIM), jnp.float32), stats,
+        ),
+        in_specs=[smem, q_spec, k_spec, k_spec, t_spec, t_spec, b_spec, m_spec],
+        out_specs=(n_spec, m_spec),
+        scratch_shapes=[pltpu.VMEM((hs, HEAD_DIM, 256), jnp.float32)],
+        compiler_params=params,
+        name="weigh_values",
+    )(
+        flags, gathered, cache_keys, cache_values, padded[0], padded[1], wide,
+        row_max.reshape(stats.shape),
+    )
+    piece = (512, HEAD_DIM)
+    attended = pl.pallas_call(
+        reduce_kernel,
+        out_shape=jax.ShapeDtypeStruct((2, *piece), jnp.bfloat16),
+        in_specs=[vmem_spec] * 2,
+        out_specs=vmem_spec,
+        scratch_shapes=[
+            pltpu.VMEM((16, *piece), jnp.float32),
+            pltpu.VMEM((8, *piece), jnp.bfloat16),
+            pltpu.VMEM((8, *piece), jnp.bfloat16),
+            pltpu.VMEM((8, *piece), jnp.bfloat16),
+            pltpu.VMEM((8, *piece), jnp.bfloat16),
+            pltpu.VMEM((TP - 1, 8, 128), jnp.float32),
+            dma((16,)), dma((16,)), dma((8,)), dma((8,)), dma((8,)), dma((8,)),
+            dma((TP,)), dma((TP,)),
+        ],
+        compiler_params=pltpu.CompilerParams(
+            collective_id=2, has_side_effects=True, vmem_limit_bytes=LIMIT
+        ),
+        name="reduce_numerators",
+    )(numerator.reshape(TP, 2, *piece), denominator.reshape(TP, 8, 128))
+    return attended.reshape(queries.shape), handed_keys, handed_values
+
 
 def solution(mesh):
+    fast = mesh.shape["tp"] == TP and mesh.shape["role"] == 1
     return jax.shard_map(
-        shards,
+        fast_shards if fast else shards,
         mesh=mesh,
         in_specs=(
             P(("groups", "role"), None, "tp"),

time: 462 us -> 169 us (0.37)
  waiting for transfers between devices: 274 us -> 0 us
  Pallas kernels: 0 us -> 149 us
  matrix products: 64.3 us -> 0 us
  other arithmetic: 44.7 us -> 3.46 us
  local copies, waits for them, and re-layouts: 49.1 us -> 12.4 us
  between operations: 14.2 us -> 0.79 us
  starting transfers between devices: 13.1 us -> 0 us
    psum x1 -> x0, waiting for transfers between devices: 172 us -> none  [shards(): summed, totals = lax.psum((flat_numerator, flat_denominator), 'tp')]
    pallas_call x0 -> x5, Pallas kernels: none -> 149 us  [the longest x1 50.7 us: fast_shards(): pl.pallas_call(reduce_kernel, out_shape=jax.ShapeDtypeStruct((2, *piece),...]
    pmax x1 -> x0, waiting for transfers between devices: 85.4 us -> none  [shards(): row_max_all = lax.pmax(jnp.stack(maxima), 'tp')]
    dot_general x12 -> x0, matrix products: 64.3 us -> none  [the longest x6 34 us: masked_scores(): jnp.einsum('qgad,kgd->gaqk', grouped, key_block, preferred_element_type=j...]
    reduce_sum x8 -> x4, other arithmetic: 31.9 us -> 2.36 us  [the longest x2 1.5 us: spans(): jnp.sum(jnp.where(t[None] == owner[:, None], counts[None], 0), axis=1)]
    unnamed x53 -> x8, local copies, waits for them, and re-layouts: 19.4 us -> 5.83 us
    all_to_all x2 -> x0, starting transfers between devices: 12.5 us -> none  [the longest x1 6.52 us: shards(): lax.all_to_all(fresh_keys, 'tp', split_axis=1, concat_axis=2, tiled=True)]
    all_gather x1 -> x0, waiting for transfers between devices: 10.9 us -> none  [shards(): gathered = lax.all_gather(queries, 'tp', axis=2, tiled=True)]
  transfers between devices with their start and end apart: 7 -> 0, of which waited for: 4 -> 0; matrix products, arithmetic and copies ran while one was open for 6% -> 0% of each run, Pallas kernels for 0% -> 0%
where the time goes in v1:
time: 169 us; the launch traced here: 166 us
  Pallas kernels  149 us (88%)
  local copies, waits for them, and re-layouts  12.4 us (7%)
  other arithmetic  3.46 us (2%)
    pallas_call x1, Pallas kernels, fast_shards(): pl.pallas_call(reduce_kernel, out_shape=jax.ShapeDtypeStruct((2, *piece),...  50.7 us
    pallas_call x1, Pallas kernels, fast_shards(): pl.pallas_call(gather_kernel, out_shape=(jax.ShapeDtypeStruct((TP, *q.sha...  34.5 us
    pallas_call x1, Pallas kernels, fast_shards(): pl.pallas_call(weigh_kernel, grid=grid, out_shape=(jax.ShapeDtypeStruct((...  27.5 us
    pallas_call x1, Pallas kernels, fast_shards(): pl.pallas_call(max_kernel, out_shape=jax.ShapeDtypeStruct((TP, 8, 128), j...  26.7 us
    pallas_call x1, Pallas kernels, fast_shards(): pl.pallas_call(local_max_kernel, grid=grid, out_shape=stats, in_specs=[sm...  9.94 us
    unnamed x8, local copies, waits for them, and re-layouts  5.83 us

profile of v1, /device:TPU:3, one launch (start us, length us, event | category | flops | bytes accessed | tf_op | source)
XLA Modules:
  0.0 166.0 jit_solution(3513941003365775110)
XLA Ops:
  0.6 0.8 select_reduce_fusion.5
  1.4 0.1 convert_reduce_fusion
  1.5 0.7 select_reduce_fusion
  2.3 0.8 select_reduce_fusion.3
  3.0 0.1 stack.49
  3.1 0.1 stack.52
  3.2 0.1 stack.50
  3.3 0.1 stack.53
  3.4 0.1 stack.55
  3.5 0.2 add_reduce_fusion
  3.7 0.1 reshape.380.flag_ref
  3.8 0.8 pad_maximum_fusion
  4.7 0.7 pad.8.f_ref
  5.3 1.8 %reshape.369.q_ref = bf16[2,512,128]{2,1,0:T(8,128)(2,1)} reshape(bf16[2,64,1024]{2,1,0:T(8,128)(2,1)} %param.8) | data formatting | bytes 524288 | tf_op jit(solution)/shard_map/reshape | solution.py:425
  7.1 0.1 broadcast_in_dim.87
  7.2 0.3 reshape.374.bound_ref
  7.5 34.5 %gather_queries.1 = (bf16[16,2,512,128]{3,2,1,0:T(8,128)(2,1)}, bf16[16,16,128]{2,1,0:T(8,128)(2,1)}) custom-call(bf16[2,512,128]{2,1,0:T(8,128)(2,1)} %reshape.369.q_ref, bf16[16,16,128]{2,1,0:T(8,128)(2,1)} %pad.8.f_ref), custom_call_target="tpu_custom_call" | custom-call | tf_op jit(solution)/shard_map/gather_queries/pallas_call | solution.py:432
  42.1 0.9 copy.31
  42.9 0.1 reshape.373
  43.0 0.1 squeeze.11
  43.1 0.6 rev.8
  43.8 0.1 squeeze.10
  43.9 0.6 rev.7
  44.5 2.2 %copy-done = bf16[16,2,512,128]{3,2,1,0:T(8,128)(2,1)S(1)} copy-done((bf16[16,2,512,128]{3,2,1,0:T(8,128)(2,1)S(1)}, bf16[16,2,512,128]{3,2,1,0:T(8,128)(2,1)}, u32[]{:S(2)}) %copy-start) | copy-done | bytes 4194328
  46.7 9.9 %local_max.1 = f32[8,2,2,4,128]{4,3,2,1,0:T(4,128)S(1)} custom-call(s32[24]{0:T(128)S(1)} %reshape.380.flag_ref, bf16[8,2,2,512,128]{4,3,2,1,0:T(8,128)(2,1)S(1)} %bitcast.37, bf16[2,1024,1024]{2,1,0:T(8,128)(2,1)} %k_ref.3, bf16[2,16,1024]{2,1,0:T(8,128)(2,1)S(1)} %get-tuple-element.19.t_ref, s32[2,4,4,256]{3,2,1,0:T(4,128)S(1)} %reshape.374.bound_ref), custom_call_target="tpu_custom_call" | custom-call | tf_op jit(solution)/shard_map/local_max/pallas_call | solution.py:484
  56.6 0.6 copy-done.3
  57.2 26.7 %row_max.1 = f32[16,8,128]{2,1,0:T(8,128)} custom-call(f32[16,8,128]{2,1,0:T(8,128)} %bitcast.40), custom_call_target="tpu_custom_call" | custom-call | tf_op jit(solution)/shard_map/row_max/pallas_call | solution.py:493
  84.0 2.2 %copy-done.1 = bf16[16,2,512,128]{3,2,1,0:T(8,128)(2,1)S(1)} copy-done((bf16[16,2,512,128]{3,2,1,0:T(8,128)(2,1)S(1)}, bf16[16,2,512,128]{3,2,1,0:T(8,128)(2,1)}, u32[]{:S(2)}) %copy-start.1) | copy-done | bytes 4194328
  86.1 0.8 copy-done.2
  87.0 27.5 %weigh_values.1 = (f32[8,2,2,512,128]{4,3,2,1,0:T(8,128)}, f32[8,2,2,4,128]{4,3,2,1,0:T(4,128)S(1)}) custom-call(s32[24]{0:T(128)S(1)} %reshape.380.flag_ref, bf16[8,2,2,512,128]{4,3,2,1,0:T(8,128)(2,1)S(1)} %bitcast.38, bf16[2,1024,1024]{2,1,0:T(8,128)(2,1)} %k_ref.3, bf16[2,1024,1024]{2,1,0:T(8,128)(2,1)} %v_ref.1, ...), custom_call_target="tpu_custom_call" | custom-call | tf_op jit(solution)/shard_map/weigh_values/pallas_call | solution.py:502
  114.5 50.7 %reduce_numerators.1 = bf16[2,512,128]{2,1,0:T(8,128)(2,1)S(1)} custom-call(f32[16,2,512,128]{3,2,1,0:T(8,128)} %bitcast.42, f32[16,8,128]{2,1,0:T(8,128)S(1)} %bitcast.41), custom_call_target="tpu_custom_call" | custom-call | tf_op jit(solution)/shard_map/reduce_numerators/pallas_call | solution.py:518
  165.2 0.8 reshape.379
  (20 shorter events, 0.1 us)
Async XLA Ops:
  44.5 2.2 %copy-start = (bf16[16,2,512,128]{3,2,1,0:T(8,128)(2,1)S(1)}, bf16[16,2,512,128]{3,2,1,0:T(8,128)(2,1)}, u32[]{:S(2)}) copy-start(bf16[16,2,512,128]{3,2,1,0:T(8,128)(2,1)} %get-tuple-element.7) | copy-start | bytes 12582916
  56.6 0.6 copy-start.3
  83.9 2.2 %copy-start.1 = (bf16[16,2,512,128]{3,2,1,0:T(8,128)(2,1)S(1)}, bf16[16,2,512,128]{3,2,1,0:T(8,128)(2,1)}, u32[]{:S(2)}) copy-start(bf16[16,2,512,128]{3,2,1,0:T(8,128)(2,1)} %get-tuple-element.7) | copy-start | bytes 12582916
  86.1 0.8 copy-start.2

commit v2 on v0

--- a/solution.py
+++ b/solution.py
@@ -1,6 +1,10 @@
+import math
+
 import jax
 import jax.numpy as jnp
 from jax import lax
+from jax.experimental import pallas as pl
+from jax.experimental.pallas import tpu as pltpu
 from jax.sharding import PartitionSpec as P
 
 HEADS = 128
@@ -136,10 +140,437 @@
     attended = shares.reshape(local_sides, query_rows, -1).astype(jnp.bfloat16)
     return (attended, handed_keys, handed_values)
 
+TP = 16
+ZS = 4
+HALF = 256
+WIDTH = 8 * 64
+TURN_PAD = 16
+SCALE = HEAD_DIM ** (-0.5) * math.log2(math.e)
+MESH = pl.DeviceIdType.MESH
+LIMIT = 56 * 1024 * 1024
+
+
+def place(z, y, c):
+    return (z * 2 + y) * 2 + c
+
+
+def greet(me):
+    barrier = pltpu.get_barrier_semaphore()
+    for d in range(1, TP):
+        pl.semaphore_signal(
+            barrier, inc=1, device_id={"tp": lax.rem(me + d, TP)}, device_id_type=MESH
+        )
+    pl.semaphore_wait(barrier, TP - 1)
+
+
+def remote(src, dst, send, recv, to):
+    return pltpu.make_async_remote_copy(
+        src_ref=src, dst_ref=dst, send_sem=send, recv_sem=recv,
+        device_id={"tp": to}, device_id_type=MESH,
+    )
+
+
+def each(count, body):
+    def step(i, carry):
+        body(i)
+        return carry
+
+    lax.fori_loop(0, count, step, 0)
+
+
+def cache_copy(cache_ref, rows_ref, sem, s, h):
+    columns = pl.ds(pl.multiple_of(h * HEAD_DIM, HEAD_DIM), HEAD_DIM)
+    count = cache_ref.shape[1]
+    return pltpu.make_async_copy(
+        cache_ref.at[s, :, columns], rows_ref.at[s, h, pl.ds(0, count), :], sem.at[s * KV_HEADS + h]
+    )
+
+
+def place_turns(turn_ref, rows_ref, values):
+    count = rows_ref.shape[2] - TURN_PAD
+
+    def body(h):
+        rows = turn_ref[2 * h].astype(jnp.float32) + turn_ref[2 * h + 1].astype(jnp.float32)
+        if values:
+            rows = jnp.concatenate([rows[8:], rows[:8]], axis=0)
+        for s in range(2):
+            rows_ref[s, h, count:, :] = rows.astype(jnp.bfloat16)
+
+    each(KV_HEADS, body)
+
+
+def masked(q_ref, qa_ref, k_ref, ka_ref, origin, s, h, part):
+    rows = slice(HALF * part, HALF * part + HALF)
+    q = jnp.concatenate([q_ref[origin, s, rows, :], qa_ref[s, rows, :]], axis=1)
+    k = jnp.concatenate([k_ref[s, h], ka_ref[s]], axis=1)
+    return lax.dot_general(
+        k, q, (((1,), (1,)), ((), ())), preferred_element_type=jnp.float32
+    )
+
+
+def gather_kernel(
+    q_ref, f_ref, keys_ref, ka_ref, qa_ref, out_ref, turn_ref, max_ref,
+    rows, local_max, slots,
+    send, recv, fsend, frecv, local, loads, msend, mrecv, gsend, grecv,
+):
+    me = lax.axis_index("tp")
+    c, y, z = lax.rem(me, 2), lax.rem(me // 2, 2), me // 4
+    other_y, other_c = place(z, 1 - y, c), place(z, y, 1 - c)
+    for s in range(2):
+        each(KV_HEADS, lambda h: cache_copy(keys_ref, rows, loads, s, h).start())
+    greet(me)
+    own = [
+        pltpu.make_async_copy(q_ref, out_ref.at[me], local.at[0]),
+        pltpu.make_async_copy(f_ref.at[me], turn_ref.at[me], local.at[1]),
+    ]
+    for copy in own:
+        copy.start()
+    fresh = []
+    for d in range(1, TP):
+        to = lax.rem(me + d, TP)
+        copy = remote(f_ref.at[to], turn_ref.at[me], fsend.at[d], frecv.at[d], to)
+        copy.start()
+        fresh.append(copy)
+
+    def push(src, origin, s, to, at):
+        remote(src, out_ref.at[origin, s], send.at[at], recv.at[origin * 2 + s], to).start()
+
+    def piece(origin, s):
+        return out_ref.at[origin, s]
+
+    def arrived(origin, s):
+        remote(
+            piece(origin, s), piece(origin, s), send.at[0], recv.at[origin * 2 + s], other_c
+        ).wait_recv()
+
+    def compute(origin, s):
+        for part in range(2):
+            scores = masked(out_ref, qa_ref, rows, ka_ref, origin, s, origin // 2, part)
+            local_max[origin, pl.ds(s, 1), HALF * part : HALF * part + HALF] = jnp.max(
+                scores, axis=0, keepdims=True
+            )
+
+    for s in range(2):
+        for n, dz in enumerate((2, 1, 3)):
+            push(q_ref.at[s], me, s, place(lax.rem(z + dz, ZS), y, c), s * 5 + n)
+        push(q_ref.at[s], me, s, other_y, s * 5 + 3)
+        push(q_ref.at[s], me, s, other_c, s * 5 + 4)
+    for d in range(1, TP):
+        fresh[d - 1].wait_recv()
+    for copy in own:
+        copy.wait()
+    place_turns(turn_ref, rows, False)
+    for s in range(2):
+        each(KV_HEADS, lambda h: cache_copy(keys_ref, rows, loads, s, h).wait())
+    each(2, lambda s: compute(me, s))
+
+    def from_z(i):
+        s = i // 3
+        origin = place(lax.rem(z + 1 + lax.rem(i, 3), ZS), y, c)
+        arrived(origin, s)
+        push(piece(origin, s), origin, s, other_y, 10 + i)
+        push(piece(origin, s), origin, s, other_c, 16 + i)
+        compute(origin, s)
+
+    each(6, from_z)
+
+    def from_y(i):
+        s = i // ZS
+        origin = place(lax.rem(z + lax.rem(i, ZS), ZS), 1 - y, c)
+        arrived(origin, s)
+        push(piece(origin, s), origin, s, other_c, 22 + i)
+        compute(origin, s)
+
+    each(8, from_y)
+
+    def from_c(i):
+        s = lax.rem(i // ZS, 2)
+        row = jnp.where(i < 8, y, 1 - y)
+        origin = place(lax.rem(z + lax.rem(i, ZS), ZS), row, 1 - c)
+        arrived(origin, s)
+        compute(origin, s)
+
+    each(16, from_c)
+    firsts, seconds = [], []
+    for d in range(1, TP):
+        to = lax.rem(me + d, TP)
+        copy = remote(local_max.at[to], slots.at[d - 1], msend.at[d], mrecv.at[d], to)
+        copy.start()
+        firsts.append(copy)
+    best = local_max[me]
+    for d in range(1, TP):
+        firsts[d - 1].wait_recv()
+        best = jnp.maximum(best, slots[d - 1])
+    max_ref[me] = best
+    for d in range(1, TP):
+        to = lax.rem(me + d, TP)
+        copy = remote(max_ref.at[me], max_ref.at[me], gsend.at[d], grecv.at[d], to)
+        copy.start()
+        seconds.append(copy)
+    each(30, lambda i: remote(
+        q_ref.at[0], out_ref.at[me, 0], send.at[i], recv.at[0], other_c
+    ).wait_send())
+    for copy in fresh + firsts:
+        copy.wait_send()
+    for copy in seconds:
+        copy.wait()
+
+
+def reduce_kernel(
+    q_ref, turn_ref, max_ref, keys_ref, values_ref, ka_ref, qa_ref, out_ref,
+    rows, vrows, num, sums, c_in, y_out, y_in, z_out, z_in, sums_in,
+    loads, vloads, c_send, c_recv, y_send, y_recv, z_send, z_recv, l_send, l_recv,
+):
+    me = lax.axis_index("tp")
+    c, y, z = lax.rem(me, 2), lax.rem(me // 2, 2), me // 4
+    other_y, other_c = place(z, 1 - y, c), place(z, y, 1 - c)
+
+    def ahead(i):
+        return jnp.where(i == 0, 2, jnp.where(i == 1, 1, jnp.where(i == 2, 3, 0)))
+
+    def chip(t):
+        row = jnp.where(t < ZS, 1 - y, y)
+        return lax.rem(z + ahead(lax.rem(t, ZS)), ZS) * 2 + row
+
+    def load(t):
+        h = chip(t)
+        return [
+            copy
+            for s in range(2)
+            for copy in (
+                cache_copy(keys_ref, rows, loads, s, h),
+                cache_copy(values_ref, vrows, vloads, s, h),
+            )
+        ]
+
+    def start_load(t):
+        for copy in load(t):
+            copy.start()
+
+    each(KV_HEADS, start_load)
+    place_turns(turn_ref, rows, False)
+    place_turns(turn_ref, vrows, True)
+    greet(me)
+
+    def c_copy(t, s):
+        at = t * 2 + s
+        return remote(
+            num.at[chip(t) * 2 + 1 - c, s], c_in.at[at], c_send.at[at], c_recv.at[at], other_c
+        )
+
+    def y_copy(t, s):
+        at = t * 2 + s
+        return remote(y_out.at[at], y_in.at[at], y_send.at[at], y_recv.at[at], other_y)
+
+    def z_copy(t, s):
+        at = t * 2 + s
+        to = place(lax.rem(z + ahead(t), ZS), y, c)
+        return remote(z_out.at[at], z_in.at[at], z_send.at[at], z_recv.at[at], to)
+
+    def compute(t):
+        h = chip(t)
+        for copy in load(t):
+            copy.wait()
+
+        def side(s):
+            v = vrows[s, h].T
+            for parity in range(2):
+                dest = 2 * h + parity
+                for part in range(2):
+                    scores = masked(q_ref, qa_ref, rows, ka_ref, dest, s, h, part)
+                    lanes = slice(HALF * part, HALF * part + HALF)
+                    top = max_ref[dest, pl.ds(s, 1), lanes]
+                    w = jnp.exp2((scores - top) * SCALE)
+                    sums[dest, pl.ds(s, 1), lanes] = jnp.sum(w, axis=0, keepdims=True)
+                    total = jnp.dot(
+                        v, w.astype(jnp.bfloat16), preferred_element_type=jnp.float32
+                    )
+                    num[dest, s, lanes, :] = total.T
+
+        each(2, side)
+        for s in range(2):
+            c_copy(t, s).start()
+
+    def pass_y(t):
+        for s in range(2):
+            c_copy(t, s).wait_recv()
+            at = t * 2 + s
+            y_out[at] = (num[chip(t) * 2 + c, s] + c_in[at]).astype(jnp.bfloat16)
+            y_copy(t, s).start()
+
+    def summed(t, s):
+        c_copy(t + ZS, s).wait_recv()
+        y_copy(t, s).wait_recv()
+        return (
+            num[chip(t + ZS) * 2 + c, s]
+            + c_in[(t + ZS) * 2 + s]
+            + y_in[t * 2 + s].astype(jnp.float32)
+        )
+
+    def pass_z(t):
+        for s in range(2):
+            z_out[t * 2 + s] = summed(t, s).astype(jnp.bfloat16)
+            z_copy(t, s).start()
+
+    def step(t):
+        compute(t)
+
+        @pl.when((t >= 1) & (t <= ZS))
+        def _():
+            pass_y(t - 1)
+
+        @pl.when(t > ZS)
+        def _():
+            pass_z(t - 1 - ZS)
+
+    each(KV_HEADS, step)
+    l_copies = []
+    for d in range(1, TP):
+        to = lax.rem(me + d, TP)
+        copy = remote(sums.at[to], sums_in.at[d - 1], l_send.at[d], l_recv.at[d], to)
+        copy.start()
+        l_copies.append(copy)
+    for s in range(2):
+        c_in[6 + s] = summed(3, s)
+    totals = sums[me]
+    for d in range(1, TP):
+        l_copies[d - 1].wait_recv()
+        totals = totals + sums_in[d - 1]
+    for s in range(2):
+        for t in range(ZS - 1):
+            z_copy(t, s).wait_recv()
+        for j in range(WIDTH // 128):
+            lanes = slice(128 * j, 128 * j + 128)
+            column = jnp.broadcast_to(totals[s : s + 1, lanes], (128, 128)).T
+            total = c_in[6 + s, lanes, :]
+            for t in range(ZS - 1):
+                total = total + z_in[t * 2 + s, lanes, :].astype(jnp.float32)
+            out_ref[s, lanes, :] = (total / column).astype(jnp.bfloat16)
+    for s in range(2):
+        each(KV_HEADS, lambda t: c_copy(t, s).wait_send())
+        each(ZS, lambda t: y_copy(t, s).wait_send())
+        each(ZS - 1, lambda t: z_copy(t, s).wait_send())
+    for copy in l_copies:
+        copy.wait_send()
+
+
+def visibility(prefill_prefixes, decode_prefixes, prefill_counts, me, query_rows, cache_rows):
+    most = decode_prefixes.shape[0]
+    turn_rows = query_rows // TP
+    t = jnp.arange(most, dtype=jnp.int32)
+    short = most - prefill_counts.shape[0]
+    lengths = jnp.stack([jnp.pad(prefill_prefixes, (0, short)), decode_prefixes])
+    counts = jnp.stack([jnp.pad(prefill_counts, (0, short)), jnp.full((most,), 2, jnp.int32)])
+    both = jnp.stack([lengths, counts])
+    ends = jnp.sum(jnp.where(t[None] <= t[:, None], both[:, :, None, :], 0), axis=-1)
+    starts = ends - both
+    at = me * cache_rows + jnp.arange(cache_rows, dtype=jnp.int32)
+    cache = (at[None, :, None] >= starts[0][:, None]) & (at[None, :, None] < ends[0][:, None])
+    cache = jnp.pad(cache, ((0, 0), (0, 0), (0, 128 - most)))
+    line = jnp.arange(TURN_PAD, dtype=jnp.int32)
+    side = jnp.arange(2, dtype=jnp.int32)[:, None]
+    column = jnp.where(
+        line[None] // turn_rows == side, most + me * turn_rows + line[None] % turn_rows, 127
+    )
+    lanes = jnp.arange(128, dtype=jnp.int32)
+    turns = column[:, :, None] == lanes
+    marks = jnp.concatenate([cache, turns], axis=1).astype(jnp.bfloat16)
+    r = jnp.arange(query_rows, dtype=jnp.int32)
+    mine = (r[None, :, None] >= starts[1][:, None]) & (r[None, :, None] < ends[1][:, None])
+    first = jnp.sum(jnp.where(mine, starts[1][:, None], 0), axis=-1)
+    j = lanes - most
+    seen = (j >= first[:, :, None]) & (j <= r[None, :, None]) & (j >= 0)
+    seen = seen | jnp.pad(mine, ((0, 0), (0, 0), (0, 128 - most)))
+    hide = jnp.where(seen, 0.0, -1e30).astype(jnp.bfloat16)
+    hide = jnp.broadcast_to(hide[:, :, None], (2, query_rows, 8, 128))
+    return marks, hide.reshape(2, query_rows * 8, 128)
+
+
+def fast_shards(
+    queries,
+    cache_keys,
+    cache_values,
+    fresh_keys,
+    fresh_values,
+    prefill_prefixes,
+    decode_prefixes,
+    prefill_counts,
+):
+    me = lax.axis_index("tp")
+    query_rows = queries.shape[1]
+    cache_rows = cache_keys.shape[1]
+    turn_rows = query_rows // TP
+    q = queries.reshape(2, query_rows * 8, HEAD_DIM)
+    fresh = jnp.stack([fresh_keys, fresh_values]).reshape(2, 2, TP, turn_rows, -1)
+    fresh = fresh.transpose(2, 0, 1, 3, 4).reshape(TP, 4 * turn_rows, -1)
+    odd = lax.rem(me, 2) == 1
+    zeros = jnp.zeros_like(fresh)
+    fresh = jnp.concatenate(
+        [jnp.where(odd, zeros, fresh), jnp.where(odd, fresh, zeros)], axis=2
+    )
+    marks, hide = visibility(
+        prefill_prefixes, decode_prefixes, prefill_counts, me, query_rows, cache_rows
+    )
+    any_spec = pl.BlockSpec(memory_space=pl.ANY)
+    vmem_spec = pl.BlockSpec(memory_space=pltpu.VMEM)
+    dma = pltpu.SemaphoreType.DMA
+    bf16, f32 = jnp.bfloat16, jnp.float32
+    all_rows = pltpu.VMEM((2, KV_HEADS, cache_rows + TURN_PAD, HEAD_DIM), bf16)
+    stats = (TP, 2, WIDTH)
+    gathered, turns, row_max = pl.pallas_call(
+        gather_kernel,
+        out_shape=(
+            jax.ShapeDtypeStruct((TP, *q.shape), bf16),
+            jax.ShapeDtypeStruct(fresh.shape, bf16),
+            jax.ShapeDtypeStruct(stats, f32),
+        ),
+        in_specs=[vmem_spec, vmem_spec, any_spec, vmem_spec, vmem_spec],
+        out_specs=(vmem_spec,) * 3,
+        scratch_shapes=[
+            all_rows, pltpu.VMEM(stats, f32), pltpu.VMEM((TP - 1, 2, WIDTH), f32),
+            dma((32,)), dma((32,)), dma((TP,)), dma((TP,)), dma((2,)), dma((16,)),
+            dma((TP,)), dma((TP,)), dma((TP,)), dma((TP,)),
+        ],
+        compiler_params=pltpu.CompilerParams(
+            collective_id=0, has_side_effects=True, vmem_limit_bytes=LIMIT
+        ),
+        name="gather_and_max",
+    )(q, fresh, cache_keys, marks, hide)
+    piece = (WIDTH, HEAD_DIM)
+    attended = pl.pallas_call(
+        reduce_kernel,
+        out_shape=jax.ShapeDtypeStruct((2, *piece), bf16),
+        in_specs=[vmem_spec] * 3 + [any_spec] * 2 + [vmem_spec] * 2,
+        out_specs=vmem_spec,
+        scratch_shapes=[
+            all_rows, all_rows,
+            pltpu.VMEM((TP, 2, *piece), f32),
+            pltpu.VMEM(stats, f32),
+            pltpu.VMEM((16, *piece), f32),
+            pltpu.VMEM((8, *piece), bf16),
+            pltpu.VMEM((8, *piece), bf16),
+            pltpu.VMEM((6, *piece), bf16),
+            pltpu.VMEM((6, *piece), bf16),
+            pltpu.VMEM((TP - 1, 2, WIDTH), f32),
+            dma((16,)), dma((16,)), dma((16,)), dma((16,)), dma((8,)), dma((8,)),
+            dma((6,)), dma((6,)), dma((TP,)), dma((TP,)),
+        ],
+        compiler_params=pltpu.CompilerParams(
+            collective_id=1, has_side_effects=True, vmem_limit_bytes=LIMIT
+        ),
+        name="weigh_and_reduce",
+    )(gathered, turns, row_max, cache_keys, cache_values, marks, hide)
+    shared = turns.reshape(KV_HEADS, 2, 2, 2, turn_rows, HEAD_DIM)
+    shared = shared[:, 0] + shared[:, 1]
+    handed = jnp.flip(shared.transpose(1, 2, 3, 0, 4), axis=1)
+    handed = handed.reshape(2, 2, turn_rows, -1)
+    return attended.reshape(queries.shape), handed[0], handed[1]
+
 
 def solution(mesh):
+    fast = mesh.shape["tp"] == TP and mesh.shape["role"] == 1
     return jax.shard_map(
-        shards,
+        fast_shards if fast else shards,
         mesh=mesh,
         in_specs=(
             P(("groups", "role"), None, "tp"),

time: 462 us -> 135 us (0.29)
  waiting for transfers between devices: 274 us -> 0 us
  Pallas kernels: 0 us -> 122 us
  matrix products: 64.3 us -> 0 us
  local copies, waits for them, and re-layouts: 49.1 us -> 6.88 us
  other arithmetic: 44.7 us -> 3.95 us
  between operations: 14.2 us -> 0.78 us
  starting transfers between devices: 13.1 us -> 0 us
    psum x1 -> x0, waiting for transfers between devices: 172 us -> none  [shards(): summed, totals = lax.psum((flat_numerator, flat_denominator), 'tp')]
    pallas_call x0 -> x2, Pallas kernels: none -> 122 us  [the longest x1 63.6 us: fast_shards(): pl.pallas_call(gather_kernel, out_shape=(jax.ShapeDtypeStruct((TP, *q.sha...]
    pmax x1 -> x0, waiting for transfers between devices: 85.4 us -> none  [shards(): row_max_all = lax.pmax(jnp.stack(maxima), 'tp')]
    dot_general x12 -> x0, matrix products: 64.3 us -> none  [the longest x6 34 us: masked_scores(): jnp.einsum('qgad,kgd->gaqk', grouped, key_block, preferred_element_type=j...]
    reduce_sum x8 -> x2, other arithmetic: 31.9 us -> 0.26 us  [the longest x1 0.15 us: visibility(): jnp.sum(jnp.where(t[None] <= t[:, None], both[:, :, None, :], 0), axis=-1)]
    unnamed x53 -> x2, local copies, waits for them, and re-layouts: 19.4 us -> 0.01 us
    all_to_all x2 -> x0, starting transfers between devices: 12.5 us -> none  [the longest x1 6.52 us: shards(): lax.all_to_all(fresh_keys, 'tp', split_axis=1, concat_axis=2, tiled=True)]
    all_gather x1 -> x0, waiting for transfers between devices: 10.9 us -> none  [shards(): gathered = lax.all_gather(queries, 'tp', axis=2, tiled=True)]
  transfers between devices with their start and end apart: 7 -> 0, of which waited for: 4 -> 0; matrix products, arithmetic and copies ran while one was open for 6% -> 0% of each run, Pallas kernels for 0% -> 0%
where the time goes in v2:
time: 135 us; the launch traced here: 134 us
  Pallas kernels  122 us (90%)
  local copies, waits for them, and re-layouts  6.88 us (5%)
  other arithmetic  3.95 us (3%)
    pallas_call x1, Pallas kernels, fast_shards(): pl.pallas_call(gather_kernel, out_shape=(jax.ShapeDtypeStruct((TP, *q.sha...  63.6 us
    pallas_call x1, Pallas kernels, fast_shards(): pl.pallas_call(reduce_kernel, out_shape=jax.ShapeDtypeStruct((2, *piece),...  58.4 us

profile of v2, /device:TPU:3, one launch (start us, length us, event | category | flops | bytes accessed | tf_op | source)
XLA Modules:
  0.0 133.6 jit_solution(12796384487843602085)
XLA Ops:
  0.6 0.7 pad_bitcast_fusion.2
  1.3 0.7 pad_bitcast_fusion.1
  2.0 0.7 add_bitcast_fusion
  2.7 0.1 iota_compare_fusion.3
  2.8 0.1 select_reduce_fusion.1
  2.9 0.1 select_reduce_fusion
  3.1 0.1 select_convert_fusion
  3.2 0.8 broadcast_select_fusion.1
  4.0 0.7 pad_maximum_fusion.1.f_ref
  4.8 0.7 broadcast_bitcast_fusion.qa_ref
  5.5 0.3 compare_and_fusion
  5.8 1.8 %reshape.158.q_ref = bf16[2,512,128]{2,1,0:T(8,128)(2,1)} reshape(bf16[2,64,1024]{2,1,0:T(8,128)(2,1)} %param.8) | data formatting | bytes 524288 | tf_op jit(solution)/shard_map/reshape | solution.py:503
  7.5 0.9 fusion.ka_ref
  8.5 63.6 %gather_and_max.1 = (bf16[16,2,512,128]{3,2,1,0:T(8,128)(2,1)}, bf16[16,16,128]{2,1,0:T(8,128)(2,1)}, f32[16,2,512]{2,1,0:T(2,128)}) custom-call(bf16[2,512,128]{2,1,0:T(8,128)(2,1)} %reshape.158.q_ref, bf16[16,16,128]{2,1,0:T(8,128)(2,1)} %pad_maximum_fusion.1.f_ref, bf16[2,1024,1024]{2,1,0:T(8,128)(2,1)} %keys_ref.3, bf16[2,1040,128]{2,1,0:T(8,128)(2,1)} %fusion.ka_ref, ...), custom_call_target="tpu_custom_call" | custom-call | tf_op jit(solution)/shard_map/gather_and_max/pallas_call | solution.py:520
  72.1 0.0 copy-start
  72.1 58.4 %weigh_and_reduce.1 = bf16[2,512,128]{2,1,0:T(8,128)(2,1)} custom-call(bf16[16,2,512,128]{3,2,1,0:T(8,128)(2,1)} %get-tuple-element.6.q_ref, bf16[16,16,128]{2,1,0:T(8,128)(2,1)} %get-tuple-element.7.turn_ref, f32[16,2,512]{2,1,0:T(2,128)} %get-tuple-element.8.max_ref, bf16[2,1024,1024]{2,1,0:T(8,128)(2,1)} %keys_ref.3, bf16[2,1024,1024]{2,1,0:T(8,128)(2,1)} %values_ref.1, ...), custom_call_target="tpu_custom_call" | custom-call | tf_op jit(solution)/shard_map/weigh_and_reduce/pallas_call | solution.py:540
  130.5 1.8 %reshape.160 = bf16[2,64,1024]{2,1,0:T(8,128)(2,1)} reshape(bf16[2,512,128]{2,1,0:T(8,128)(2,1)} %weigh_and_reduce.1) | data formatting | bytes 524288 | tf_op jit(solution)/shard_map/reshape | solution.py:567
  132.2 0.0 copy-done
  132.3 0.6 squeeze.9
  133.0 0.6 squeeze.8
  (18 shorter events, 0.1 us)
Async XLA Ops:
  72.1 60.2 %copy-start = (bf16[16,16,128]{2,1,0:T(8,128)(2,1)S(1)}, bf16[16,16,128]{2,1,0:T(8,128)(2,1)}, u32[]{:S(2)}) copy-start(bf16[16,16,128]{2,1,0:T(8,128)(2,1)} %get-tuple-element.7.turn_ref) | copy-start | bytes 196612

commit v3 on v2

--- a/solution.py
+++ b/solution.py
@@ -208,16 +208,20 @@
     )
 
 
-def gather_kernel(
-    q_ref, f_ref, keys_ref, ka_ref, qa_ref, out_ref, turn_ref, max_ref,
-    rows, local_max, slots,
-    send, recv, fsend, frecv, local, loads, msend, mrecv, gsend, grecv,
+def attend_kernel(
+    q_ref, f_ref, keys_ref, values_ref, ka_ref, qa_ref, attended_ref, turn_ref,
+    out_ref, max_ref, rows, vrows, local_max, slots,
+    num, sums, c_in, y_out, y_in, z_out, z_in, sums_in,
+    send, recv, fsend, frecv, local, loads, vloads, msend, mrecv, gsend, grecv,
+    c_send, c_recv, y_send, y_recv, z_send, z_recv, l_send, l_recv,
 ):
     me = lax.axis_index("tp")
     c, y, z = lax.rem(me, 2), lax.rem(me // 2, 2), me // 4
     other_y, other_c = place(z, 1 - y, c), place(z, y, 1 - c)
     for s in range(2):
         each(KV_HEADS, lambda h: cache_copy(keys_ref, rows, loads, s, h).start())
+    for s in range(2):
+        each(KV_HEADS, lambda h: cache_copy(values_ref, vrows, vloads, s, h).start())
     greet(me)
     own = [
         pltpu.make_async_copy(q_ref, out_ref.at[me], local.at[0]),
@@ -250,6 +254,10 @@
                 scores, axis=0, keepdims=True
             )
 
+    def max_copy(d):
+        to = lax.rem(me + d, TP)
+        return remote(local_max.at[to], slots.at[d - 1], msend.at[d], mrecv.at[d], to)
+
     for s in range(2):
         for n, dz in enumerate((2, 1, 3)):
             push(q_ref.at[s], me, s, place(lax.rem(z + dz, ZS), y, c), s * 5 + n)
@@ -260,46 +268,57 @@
     for copy in own:
         copy.wait()
     place_turns(turn_ref, rows, False)
+    place_turns(turn_ref, vrows, True)
     for s in range(2):
         each(KV_HEADS, lambda h: cache_copy(keys_ref, rows, loads, s, h).wait())
     each(2, lambda s: compute(me, s))
 
+    def nearest(i):
+        return jnp.where(i == 2, 3, jnp.where(i == 3, 2, i))
+
     def from_z(i):
         s = i // 3
-        origin = place(lax.rem(z + 1 + lax.rem(i, 3), ZS), y, c)
+        origin = place(lax.rem(z + nearest(1 + lax.rem(i, 3)), ZS), y, c)
         arrived(origin, s)
         push(piece(origin, s), origin, s, other_y, 10 + i)
         push(piece(origin, s), origin, s, other_c, 16 + i)
         compute(origin, s)
 
+        @pl.when(i >= 3)
+        def _():
+            max_copy(lax.rem(origin - me + TP, TP)).start()
+
     each(6, from_z)
 
     def from_y(i):
         s = i // ZS
-        origin = place(lax.rem(z + lax.rem(i, ZS), ZS), 1 - y, c)
+        origin = place(lax.rem(z + nearest(lax.rem(i, ZS)), ZS), 1 - y, c)
         arrived(origin, s)
         push(piece(origin, s), origin, s, other_c, 22 + i)
         compute(origin, s)
 
+        @pl.when(i >= ZS)
+        def _():
+            max_copy(lax.rem(origin - me + TP, TP)).start()
+
     each(8, from_y)
 
     def from_c(i):
         s = lax.rem(i // ZS, 2)
         row = jnp.where(i < 8, y, 1 - y)
-        origin = place(lax.rem(z + lax.rem(i, ZS), ZS), row, 1 - c)
+        origin = place(lax.rem(z + nearest(lax.rem(i, ZS)), ZS), row, 1 - c)
         arrived(origin, s)
         compute(origin, s)
 
+        @pl.when(lax.rem(i // ZS, 2) == 1)
+        def _():
+            max_copy(lax.rem(origin - me + TP, TP)).start()
+
     each(16, from_c)
-    firsts, seconds = [], []
-    for d in range(1, TP):
-        to = lax.rem(me + d, TP)
-        copy = remote(local_max.at[to], slots.at[d - 1], msend.at[d], mrecv.at[d], to)
-        copy.start()
-        firsts.append(copy)
+    seconds = []
     best = local_max[me]
     for d in range(1, TP):
-        firsts[d - 1].wait_recv()
+        max_copy(d).wait_recv()
         best = jnp.maximum(best, slots[d - 1])
     max_ref[me] = best
     for d in range(1, TP):
@@ -310,47 +329,19 @@
     each(30, lambda i: remote(
         q_ref.at[0], out_ref.at[me, 0], send.at[i], recv.at[0], other_c
     ).wait_send())
-    for copy in fresh + firsts:
+    for copy in fresh:
         copy.wait_send()
+    for d in range(1, TP):
+        max_copy(d).wait_send()
     for copy in seconds:
         copy.wait()
 
-
-def reduce_kernel(
-    q_ref, turn_ref, max_ref, keys_ref, values_ref, ka_ref, qa_ref, out_ref,
-    rows, vrows, num, sums, c_in, y_out, y_in, z_out, z_in, sums_in,
-    loads, vloads, c_send, c_recv, y_send, y_recv, z_send, z_recv, l_send, l_recv,
-):
-    me = lax.axis_index("tp")
-    c, y, z = lax.rem(me, 2), lax.rem(me // 2, 2), me // 4
-    other_y, other_c = place(z, 1 - y, c), place(z, y, 1 - c)
-
     def ahead(i):
         return jnp.where(i == 0, 2, jnp.where(i == 1, 1, jnp.where(i == 2, 3, 0)))
 
     def chip(t):
-        row = jnp.where(t < ZS, 1 - y, y)
-        return lax.rem(z + ahead(lax.rem(t, ZS)), ZS) * 2 + row
-
-    def load(t):
-        h = chip(t)
-        return [
-            copy
-            for s in range(2)
-            for copy in (
-                cache_copy(keys_ref, rows, loads, s, h),
-                cache_copy(values_ref, vrows, vloads, s, h),
-            )
-        ]
-
-    def start_load(t):
-        for copy in load(t):
-            copy.start()
-
-    each(KV_HEADS, start_load)
-    place_turns(turn_ref, rows, False)
-    place_turns(turn_ref, vrows, True)
-    greet(me)
+        row = jnp.where(lax.rem(t, 2) == 0, 1 - y, y)
+        return lax.rem(z + ahead(t // 2), ZS) * 2 + row
 
     def c_copy(t, s):
         at = t * 2 + s
@@ -369,15 +360,15 @@
 
     def compute(t):
         h = chip(t)
-        for copy in load(t):
-            copy.wait()
+        for s in range(2):
+            cache_copy(values_ref, vrows, vloads, s, h).wait()
 
         def side(s):
             v = vrows[s, h].T
             for parity in range(2):
                 dest = 2 * h + parity
                 for part in range(2):
-                    scores = masked(q_ref, qa_ref, rows, ka_ref, dest, s, h, part)
+                    scores = masked(out_ref, qa_ref, rows, ka_ref, dest, s, h, part)
                     lanes = slice(HALF * part, HALF * part + HALF)
                     top = max_ref[dest, pl.ds(s, 1), lanes]
                     w = jnp.exp2((scores - top) * SCALE)
@@ -393,17 +384,17 @@
 
     def pass_y(t):
         for s in range(2):
-            c_copy(t, s).wait_recv()
-            at = t * 2 + s
-            y_out[at] = (num[chip(t) * 2 + c, s] + c_in[at]).astype(jnp.bfloat16)
+            c_copy(2 * t, s).wait_recv()
+            partial = num[chip(2 * t) * 2 + c, s] + c_in[4 * t + s]
+            y_out[t * 2 + s] = partial.astype(jnp.bfloat16)
             y_copy(t, s).start()
 
     def summed(t, s):
-        c_copy(t + ZS, s).wait_recv()
+        c_copy(2 * t + 1, s).wait_recv()
         y_copy(t, s).wait_recv()
         return (
-            num[chip(t + ZS) * 2 + c, s]
-            + c_in[(t + ZS) * 2 + s]
+            num[chip(2 * t + 1) * 2 + c, s]
+            + c_in[4 * t + 2 + s]
             + y_in[t * 2 + s].astype(jnp.float32)
         )
 
@@ -413,17 +404,15 @@
             z_copy(t, s).start()
 
     def step(t):
-        compute(t)
-
-        @pl.when((t >= 1) & (t <= ZS))
+        compute(2 * t)
+        compute(2 * t + 1)
+        pass_y(t)
+
+        @pl.when(t >= 1)
         def _():
-            pass_y(t - 1)
-
-        @pl.when(t > ZS)
-        def _():
-            pass_z(t - 1 - ZS)
-
-    each(KV_HEADS, step)
+            pass_z(t - 1)
+
+    each(ZS, step)
     l_copies = []
     for d in range(1, TP):
         to = lax.rem(me + d, TP)
@@ -445,7 +434,7 @@
             total = c_in[6 + s, lanes, :]
             for t in range(ZS - 1):
                 total = total + z_in[t * 2 + s, lanes, :].astype(jnp.float32)
-            out_ref[s, lanes, :] = (total / column).astype(jnp.bfloat16)
+            attended_ref[s, lanes, :] = (total / column).astype(jnp.bfloat16)
     for s in range(2):
         each(KV_HEADS, lambda t: c_copy(t, s).wait_send())
         each(ZS, lambda t: y_copy(t, s).wait_send())
@@ -517,33 +506,19 @@
     bf16, f32 = jnp.bfloat16, jnp.float32
     all_rows = pltpu.VMEM((2, KV_HEADS, cache_rows + TURN_PAD, HEAD_DIM), bf16)
     stats = (TP, 2, WIDTH)
-    gathered, turns, row_max = pl.pallas_call(
-        gather_kernel,
+    piece = (WIDTH, HEAD_DIM)
+    attended, turns = pl.pallas_call(
+        attend_kernel,
         out_shape=(
-            jax.ShapeDtypeStruct((TP, *q.shape), bf16),
+            jax.ShapeDtypeStruct((2, *piece), bf16),
             jax.ShapeDtypeStruct(fresh.shape, bf16),
-            jax.ShapeDtypeStruct(stats, f32),
         ),
-        in_specs=[vmem_spec, vmem_spec, any_spec, vmem_spec, vmem_spec],
-        out_specs=(vmem_spec,) * 3,
+        in_specs=[vmem_spec, vmem_spec, any_spec, any_spec, vmem_spec, vmem_spec],
+        out_specs=(vmem_spec,) * 2,
         scratch_shapes=[
-            all_rows, pltpu.VMEM(stats, f32), pltpu.VMEM((TP - 1, 2, WIDTH), f32),
-            dma((32,)), dma((32,)), dma((TP,)), dma((TP,)), dma((2,)), dma((16,)),
-            dma((TP,)), dma((TP,)), dma((TP,)), dma((TP,)),
-        ],
-        compiler_params=pltpu.CompilerParams(
-            collective_id=0, has_side_effects=True, vmem_limit_bytes=LIMIT
-        ),
-        name="gather_and_max",
-    )(q, fresh, cache_keys, marks, hide)
-    piece = (WIDTH, HEAD_DIM)
-    attended = pl.pallas_call(
-        reduce_kernel,
-        out_shape=jax.ShapeDtypeStruct((2, *piece), bf16),
-        in_specs=[vmem_spec] * 3 + [any_spec] * 2 + [vmem_spec] * 2,
-        out_specs=vmem_spec,
-        scratch_shapes=[
+            pltpu.VMEM((TP, *q.shape), bf16), pltpu.VMEM(stats, f32),
             all_rows, all_rows,
+            pltpu.VMEM(stats, f32), pltpu.VMEM((TP - 1, 2, WIDTH), f32),
             pltpu.VMEM((TP, 2, *piece), f32),
             pltpu.VMEM(stats, f32),
             pltpu.VMEM((16, *piece), f32),
@@ -552,14 +527,16 @@
             pltpu.VMEM((6, *piece), bf16),
             pltpu.VMEM((6, *piece), bf16),
             pltpu.VMEM((TP - 1, 2, WIDTH), f32),
-            dma((16,)), dma((16,)), dma((16,)), dma((16,)), dma((8,)), dma((8,)),
+            dma((32,)), dma((32,)), dma((TP,)), dma((TP,)), dma((2,)), dma((16,)),
+            dma((16,)), dma((TP,)), dma((TP,)), dma((TP,)), dma((TP,)),
+            dma((16,)), dma((16,)), dma((8,)), dma((8,)),
             dma((6,)), dma((6,)), dma((TP,)), dma((TP,)),
         ],
         compiler_params=pltpu.CompilerParams(
-            collective_id=1, has_side_effects=True, vmem_limit_bytes=LIMIT
+            collective_id=0, has_side_effects=True, vmem_limit_bytes=LIMIT
         ),
-        name="weigh_and_reduce",
-    )(gathered, turns, row_max, cache_keys, cache_values, marks, hide)
+        name="attend",
+    )(q, fresh, cache_keys, cache_values, marks, hide)
     shared = turns.reshape(KV_HEADS, 2, 2, 2, turn_rows, HEAD_DIM)
     shared = shared[:, 0] + shared[:, 1]
     handed = jnp.flip(shared.transpose(1, 2, 3, 0, 4), axis=1)

time: 135 us -> 120 us (0.89)
  Pallas kernels: 122 us -> 106 us
    pallas_call x2 -> x1, Pallas kernels: 122 us -> 106 us  [fast_shards(): pl.pallas_call(attend_kernel, out_shape=(jax.ShapeDtypeStruct((2, *piece)...]
where the time goes in v3:
time: 120 us; the launch traced here: 118 us
  Pallas kernels  106 us (88%)
  local copies, waits for them, and re-layouts  6.86 us (6%)
  other arithmetic  4.71 us (4%)
    pallas_call x1, Pallas kernels, fast_shards(): pl.pallas_call(attend_kernel, out_shape=(jax.ShapeDtypeStruct((2, *piece)...  106 us

profile of v3, /device:TPU:3, one launch (start us, length us, event | category | flops | bytes accessed | tf_op | source)
XLA Modules:
  0.0 118.3 jit_solution(7428988657276684120)
XLA Ops:
  0.6 0.7 pad_bitcast_fusion.2
  1.3 0.7 pad_bitcast_fusion.1
  2.0 0.7 add_bitcast_fusion
  2.7 0.1 iota_compare_fusion.3
  2.8 0.1 select_reduce_fusion.1
  2.9 0.1 select_reduce_fusion
  3.1 0.1 select_convert_fusion
  3.2 0.8 broadcast_select_fusion.1
  4.0 0.7 pad_maximum_fusion.1.f_ref
  4.8 0.7 broadcast_bitcast_fusion.qa_ref
  5.5 0.3 compare_and_fusion
  5.8 1.8 %reshape.158.q_ref = bf16[2,512,128]{2,1,0:T(8,128)(2,1)} reshape(bf16[2,64,1024]{2,1,0:T(8,128)(2,1)} %param.8) | data formatting | bytes 524288 | tf_op jit(solution)/shard_map/reshape | solution.py:492
  7.5 0.9 fusion.ka_ref
  8.5 105.9 %attend.1 = (bf16[2,512,128]{2,1,0:T(8,128)(2,1)}, bf16[16,16,128]{2,1,0:T(8,128)(2,1)}) custom-call(bf16[2,512,128]{2,1,0:T(8,128)(2,1)} %reshape.158.q_ref, bf16[16,16,128]{2,1,0:T(8,128)(2,1)} %pad_maximum_fusion.1.f_ref, bf16[2,1024,1024]{2,1,0:T(8,128)(2,1)} %keys_ref.1, bf16[2,1024,1024]{2,1,0:T(8,128)(2,1)} %values_ref.1, ...), custom_call_target="tpu_custom_call" | custom-call | tf_op jit(solution)/shard_map/attend/pallas_call | solution.py:510
  114.4 1.8 %reshape.160 = bf16[2,64,1024]{2,1,0:T(8,128)(2,1)} reshape(bf16[2,512,128]{2,1,0:T(8,128)(2,1)} %get-tuple-element.5) | data formatting | bytes 524288 | tf_op jit(solution)/shard_map/reshape | solution.py:544
  116.2 0.8 fusion.2
  117.0 0.6 squeeze.9
  117.6 0.6 squeeze.8
  (17 shorter events, 0.1 us)

commit v4 on v3

--- a/solution.py
+++ b/solution.py
@@ -288,33 +288,31 @@
         def _():
             max_copy(lax.rem(origin - me + TP, TP)).start()
 
-    each(6, from_z)
-
-    def from_y(i):
-        s = i // ZS
-        origin = place(lax.rem(z + nearest(lax.rem(i, ZS)), ZS), 1 - y, c)
-        arrived(origin, s)
-        push(piece(origin, s), origin, s, other_c, 22 + i)
+    def along(i):
+        return lax.rem(z + nearest(i), ZS)
+
+    def finish(origin, s):
         compute(origin, s)
 
-        @pl.when(i >= ZS)
+        @pl.when(s == 1)
         def _():
             max_copy(lax.rem(origin - me + TP, TP)).start()
 
-    each(8, from_y)
-
-    def from_c(i):
-        s = lax.rem(i // ZS, 2)
-        row = jnp.where(i < 8, y, 1 - y)
-        origin = place(lax.rem(z + nearest(lax.rem(i, ZS)), ZS), row, 1 - c)
+    def take_y(origin, s, at):
         arrived(origin, s)
-        compute(origin, s)
-
-        @pl.when(lax.rem(i // ZS, 2) == 1)
-        def _():
-            max_copy(lax.rem(origin - me + TP, TP)).start()
-
-    each(16, from_c)
+        push(piece(origin, s), origin, s, other_c, at)
+        finish(origin, s)
+
+    def take_c(origin, s):
+        arrived(origin, s)
+        finish(origin, s)
+
+    each(2, lambda s: take_y(other_y, s, 22 + s))
+    each(2, lambda s: take_c(other_c, s))
+    each(6, from_z)
+    each(6, lambda i: take_y(place(along(1 + lax.rem(i, 3)), 1 - y, c), i // 3, 24 + i))
+    each(6, lambda i: take_c(place(along(1 + lax.rem(i, 3)), y, 1 - c), i // 3))
+    each(8, lambda i: take_c(place(along(lax.rem(i, ZS)), 1 - y, 1 - c), i // ZS))
     seconds = []
     best = local_max[me]
     for d in range(1, TP):
@@ -333,8 +331,6 @@
         copy.wait_send()
     for d in range(1, TP):
         max_copy(d).wait_send()
-    for copy in seconds:
-        copy.wait()
 
     def ahead(i):
         return jnp.where(i == 0, 2, jnp.where(i == 1, 1, jnp.where(i == 2, 3, 0)))
@@ -362,6 +358,15 @@
         h = chip(t)
         for s in range(2):
             cache_copy(values_ref, vrows, vloads, s, h).wait()
+        for core in range(2):
+            src = 2 * h + core
+            d = lax.rem(me - src + TP, TP)
+
+            @pl.when(d != 0)
+            def _():
+                remote(
+                    max_ref.at[src], max_ref.at[src], gsend.at[d], grecv.at[d], other_c
+                ).wait_recv()
 
         def side(s):
             v = vrows[s, h].T
@@ -439,7 +444,7 @@
         each(KV_HEADS, lambda t: c_copy(t, s).wait_send())
         each(ZS, lambda t: y_copy(t, s).wait_send())
         each(ZS - 1, lambda t: z_copy(t, s).wait_send())
-    for copy in l_copies:
+    for copy in l_copies + seconds:
         copy.wait_send()
 
 

time: 120 us -> 119 us (level)
  no operation moved by 1% of the time
where the time goes in v4:
time: 119 us; the launch traced here: 117 us
  Pallas kernels  105 us (88%)
  local copies, waits for them, and re-layouts  6.86 us (6%)
  other arithmetic  4.71 us (4%)
    pallas_call x1, Pallas kernels, fast_shards(): pl.pallas_call(attend_kernel, out_shape=(jax.ShapeDtypeStruct((2, *piece)...  105 us

profile of v4, /device:TPU:3, one launch (start us, length us, event | category | flops | bytes accessed | tf_op | source)
XLA Modules:
  0.0 117.1 jit_solution(6891043106365417484)
XLA Ops:
  0.6 0.7 pad_bitcast_fusion.2
  1.3 0.7 pad_bitcast_fusion.1
  2.0 0.7 add_bitcast_fusion
  2.7 0.1 iota_compare_fusion.3
  2.8 0.1 select_reduce_fusion.1
  2.9 0.1 select_reduce_fusion
  3.1 0.1 select_convert_fusion
  3.2 0.8 broadcast_select_fusion.1
  4.0 0.7 pad_maximum_fusion.1.f_ref
  4.8 0.7 broadcast_bitcast_fusion.qa_ref
  5.5 0.3 compare_and_fusion
  5.8 1.8 %reshape.158.q_ref = bf16[2,512,128]{2,1,0:T(8,128)(2,1)} reshape(bf16[2,64,1024]{2,1,0:T(8,128)(2,1)} %param.8) | data formatting | bytes 524288 | tf_op jit(solution)/shard_map/reshape | solution.py:497
  7.5 0.9 fusion.ka_ref
  8.5 104.7 %attend.1 = (bf16[2,512,128]{2,1,0:T(8,128)(2,1)}, bf16[16,16,128]{2,1,0:T(8,128)(2,1)}) custom-call(bf16[2,512,128]{2,1,0:T(8,128)(2,1)} %reshape.158.q_ref, bf16[16,16,128]{2,1,0:T(8,128)(2,1)} %pad_maximum_fusion.1.f_ref, bf16[2,1024,1024]{2,1,0:T(8,128)(2,1)} %keys_ref.1, bf16[2,1024,1024]{2,1,0:T(8,128)(2,1)} %values_ref.1, ...), custom_call_target="tpu_custom_call" | custom-call | tf_op jit(solution)/shard_map/attend/pallas_call | solution.py:515
  113.2 1.8 %reshape.160 = bf16[2,64,1024]{2,1,0:T(8,128)(2,1)} reshape(bf16[2,512,128]{2,1,0:T(8,128)(2,1)} %get-tuple-element.5) | data formatting | bytes 524288 | tf_op jit(solution)/shard_map/reshape | solution.py:549
  115.0 0.8 fusion.2
  115.8 0.6 squeeze.9
  116.5 0.6 squeeze.8
  (17 shorter events, 0.1 us)
